TPU v7x, 32 devices: a whole 2x2x4 slice. The times are simulated.
32 devices in a mesh: dp: 4 (over z), expert: 2 (over y), tensor: 4 (over x, core).
Axes of the slice: x: 2, y: 2, z: 4, core: 2. Of those that a mesh axis runs over, the one named last changes fastest.
Arguments:
- tokens: bfloat16 [512, 6144], P(('dp', 'expert', 'tensor')), may hold values from -6 to 6
- expert_ids: int32 [512, 2], P(('dp', 'expert', 'tensor')), may hold values from 0 to 7, all different within a row; in each aligned block of 16 rows (0 to 15, 16 to 31, ...) at most 8 rows name the same one
- gate_values: float32 [512, 2], P(('dp', 'expert', 'tensor')), may hold values from 0.25 to 1
- w_gate: bfloat16 [2, 6144, 8192], P('expert', 'dp', 'tensor'), may hold values from -0.078125 to 0.078125
- w_up: bfloat16 [2, 6144, 8192], P('expert', 'dp', 'tensor'), may hold values from -0.078125 to 0.078125
- w_down: bfloat16 [2, 8192, 6144], P('expert', 'tensor', 'dp'), may hold values from -0.0625 to 0.0625
- grad_out: bfloat16 [512, 6144], P(('dp', 'expert', 'tensor')), may hold values from -6 to 6
Outputs:
- mixed: bfloat16 [512, 6144], P(('dp', 'expert', 'tensor'))
- grad_tokens: bfloat16 [512, 6144], P(('dp', 'expert', 'tensor'))
- grad_gate: float32 [2, 6144, 8192], P('expert', 'dp', 'tensor')
- grad_up: float32 [2, 6144, 8192], P('expert', 'dp', 'tensor')
- grad_down: float32 [2, 8192, 6144], P('expert', 'tensor', 'dp')
Inputs may be any that keep to these rules, and one draw needn't show every extreme that they name: `expert_ids`: each row names two different experts; in the rows of one device no expert is named by more than 8 rows.
All inputs are finite; a program needn't handle non-finite values.
Results may differ from a plain program's by a relative error of at most 0.022.
Values may be sent and summed in bfloat16 or wider, within the bound.
A program may use at most 128 MiB of HBM per device.

v0:
```python
import jax
import jax.numpy as jnp
from jax import lax
from jax.sharding import PartitionSpec as P


def spread(send_rows):
    moved = lax.all_to_all(
        lax.all_to_all(send_rows, "dp", split_axis=2, concat_axis=1, tiled=True),
        "expert",
        split_axis=0,
        concat_axis=0,
        tiled=True,
    )
    flat = moved.reshape(-1, moved.shape[2])
    return lax.all_gather(flat, "tensor", axis=0, tiled=True)


def width_sums(term_fn, total_rows):
    return lax.psum_scatter(
        term_fn(jnp.int32(0), total_rows // lax.axis_size("dp") * lax.axis_size("dp")).astype(
            jnp.bfloat16
        ),
        "dp",
        scatter_dimension=0,
        tiled=True,
    ).astype(jnp.float32)


def gather_rows(values):
    return lax.all_gather(values, "dp", axis=0, tiled=True)


def collect(partial_rows, n_exp, cap):
    n_dp = lax.axis_size("dp")
    quarter = partial_rows.shape[1]
    summed = lax.psum_scatter(
        partial_rows.astype(jnp.bfloat16), "tensor", scatter_dimension=0, tiled=True
    )
    local = summed.reshape(n_exp, n_dp * cap, quarter)
    return lax.all_to_all(
        lax.all_to_all(local, "dp", split_axis=1, concat_axis=2, tiled=True),
        "expert",
        split_axis=0,
        concat_axis=0,
        tiled=True,
    )


def body(tokens, expert_ids, gate_values, w_gate, w_up, w_down, grad_out):
    tok_rows = tokens.shape[0]
    cap = tok_rows // 2
    n_exp = lax.axis_size("expert")
    gate_mat = w_gate[0]
    up_mat = w_up[0]
    down_mat = w_down[0]
    hidden_width = gate_mat.shape[1]
    slots = jnp.arange(cap, dtype=jnp.int32)
    selector_list = []
    weight_list = []
    for expert in range(n_exp):
        chosen = (expert_ids == expert).astype(jnp.int32)
        flat_chosen = chosen.reshape(-1)
        ranks = jnp.cumsum(flat_chosen) - 1
        onehot = ((ranks[:, None] == slots[None, :]) & (flat_chosen[:, None] > 0)).astype(
            jnp.float32
        )
        selector_list.append(jnp.sum(onehot.reshape(tok_rows, 2, cap), axis=1).T)
        weight_list.append(jnp.sum(gate_values * chosen.astype(jnp.float32), axis=1))
    selector = jnp.stack(selector_list)
    weights = jnp.stack(weight_list)
    selector_bf = selector.astype(jnp.bfloat16)
    send_rows = jnp.einsum(
        "wct,td->wcd", selector_bf, tokens, preferred_element_type=jnp.float32
    ).astype(jnp.bfloat16)
    panel_rows = spread(send_rows)
    total_rows = panel_rows.shape[0]

    def forward_term(start, count):
        gate_part = jnp.dot(panel_rows, gate_mat, preferred_element_type=jnp.float32)
        up_part = jnp.dot(panel_rows, up_mat, preferred_element_type=jnp.float32)
        return jnp.concatenate([gate_part, up_part], axis=1)

    sums = width_sums(forward_term, total_rows)
    gate = sums[:, :hidden_width]
    upper = sums[:, hidden_width:]
    sigma = jax.nn.sigmoid(gate)
    active = gate * sigma
    hidden = (active * upper).astype(jnp.bfloat16)
    hidden_all = gather_rows(hidden)
    out_partial = jnp.dot(hidden_all, down_mat, preferred_element_type=jnp.float32)
    out_home = collect(out_partial, n_exp, cap)
    weighted = selector * weights[:, None, :]
    mixed = jnp.einsum(
        "wct,wcd->td", weighted, out_home.astype(jnp.float32), precision=lax.Precision.HIGHEST
    ).astype(jnp.bfloat16)
    scaled = (weights[:, :, None] * grad_out.astype(jnp.float32)[None]).astype(jnp.bfloat16)
    send_grads = jnp.einsum(
        "wct,wtd->wcd", selector_bf, scaled, preferred_element_type=jnp.float32
    ).astype(jnp.bfloat16)
    grad_panels = spread(send_grads)

    def backward_term(start, count):
        return lax.dot_general(
            grad_panels, down_mat, (((1,), (1,)), ((), ())), preferred_element_type=jnp.float32
        )

    dhidden = width_sums(backward_term, total_rows)
    dgate = (dhidden * upper * sigma * (1.0 + gate * (1.0 - sigma))).astype(jnp.bfloat16)
    dup = (dhidden * active).astype(jnp.bfloat16)
    both_rows = jnp.concatenate([dgate, dup], axis=1)
    both_all = gather_rows(both_rows)
    dgate_all = both_all[:, :hidden_width]
    dup_all = both_all[:, hidden_width:]
    grad_down = lax.dot_general(
        hidden_all, grad_panels, (((0,), (0,)), ((), ())), preferred_element_type=jnp.float32
    )
    grad_gate = lax.dot_general(
        panel_rows, dgate_all, (((0,), (0,)), ((), ())), preferred_element_type=jnp.float32
    )
    grad_up = lax.dot_general(
        panel_rows, dup_all, (((0,), (0,)), ((), ())), preferred_element_type=jnp.float32
    )
    dx_partial = lax.dot_general(
        dgate_all, gate_mat, (((1,), (1,)), ((), ())), preferred_element_type=jnp.float32
    )
    dx_partial = dx_partial + lax.dot_general(
        dup_all, up_mat, (((1,), (1,)), ((), ())), preferred_element_type=jnp.float32
    )
    back_home = collect(dx_partial, n_exp, cap)
    grad_tokens = jnp.einsum(
        "wct,wcd->td", selector, back_home.astype(jnp.float32), precision=lax.Precision.HIGHEST
    ).astype(jnp.bfloat16)
    return (mixed, grad_tokens, grad_gate[None], grad_up[None], grad_down[None])


def solution(mesh):
    return jax.shard_map(
        body,
        mesh=mesh,
        in_specs=(
            P(("dp", "expert", "tensor"), None),
            P(("dp", "expert", "tensor"), None),
            P(("dp", "expert", "tensor"), None),
            P("expert", "dp", "tensor"),
            P("expert", "dp", "tensor"),
            P("expert", "tensor", "dp"),
            P(("dp", "expert", "tensor"), None),
        ),
        out_specs=(
            P(("dp", "expert", "tensor"), None),
            P(("dp", "expert", "tensor"), None),
            P("expert", "dp", "tensor"),
            P("expert", "dp", "tensor"),
            P("expert", "tensor", "dp"),
        ),
        check_vma=False,
    )
```

profile of v0, /device:TPU:0, one launch (start us, length us, event | category | flops | bytes accessed | tf_op | source)
XLA Modules:
  0.0 307.3 jit_solution(14486839358606379803)
XLA Ops:
  7.2 0.0 reduce-scatter.5.cloned.1.call-start
  7.2 0.7 broadcast_compare_fusion.1
  7.9 0.1 copy.67
  8.0 0.1 reshape.97
  8.1 0.1 reduce-window.9
  8.2 0.1 add_reduce_fusion
  8.3 0.1 sub.16
  8.4 0.1 copy.69
  8.4 0.1 copy.64
  8.5 0.1 reshape.96
  8.6 0.1 reduce-window.6
  8.7 0.1 add_reduce_fusion.1
  8.8 0.1 sub.14
  8.9 0.1 copy.66
  9.0 0.2 convolution_convert_fusion.1
  9.2 4.0 %copy.70 = bf16[2,8,6144]{1,0,2:T(2,128)(2,1)S(1)} copy(bf16[2,8,6144]{2,1,0:T(8,128)(2,1)S(1)} %convolution_convert_fusion.1) | data formatting | bytes 393216 | tf_op jit(solution)/shard_map/convert_element_type | solution.py:75
  13.2 3.4 %reshape.100 = bf16[4,2,12288]{2,1,0:T(2,128)(2,1)S(1)} reshape(bf16[6144,2,8]{2,1,0:T(2,128)(2,1)S(1)} %bitcast.88) | data formatting | bytes 393216
  16.6 13.6 %all_to_all.92 = bf16[4,2,12288]{2,1,0:T(2,128)(2,1)S(1)} all-to-all(bf16[4,2,12288]{2,1,0:T(2,128)(2,1)S(1)} %reshape.100), channel_id=1, replica_groups=mesh['dp'=4,'expert'=2,'tensor'=4] {'dp'}, dimensions={0} | all-to-all | bytes 393216 | tf_op jit(solution)/shard_map/all_to_all | solution.py:9
  30.2 3.7 %reshape.101 = bf16[6144,2,8]{2,1,0:T(2,128)(2,1)S(1)} reshape(bf16[4,2,12288]{2,1,0:T(2,128)(2,1)S(1)} %all_to_all.92) | data formatting | bytes 393216
  33.9 2.0 copy.80
  36.0 7.4 %all_to_all.93 = bf16[2,32,1536]{2,1,0:T(8,128)(2,1)S(1)} all-to-all(bf16[2,32,1536]{2,1,0:T(8,128)(2,1)S(1)} %bitcast.96), channel_id=1, replica_groups=mesh['dp'=4,'expert'=2,'tensor'=4] {'expert'}, dimensions={0} | all-to-all | bytes 393216 | tf_op jit(solution)/shard_map/all_to_all | solution.py:8
  43.4 8.7 %all_gather.12 = bf16[256,1536]{1,0:T(8,128)(2,1)S(1)} all-gather(bf16[64,1536]{1,0:T(8,128)(2,1)S(1)} %bitcast.98), channel_id=1, replica_groups=mesh['dp'=4,'expert'=2,'tensor'=4] {'tensor'}, dimensions={0}, use_global_device_ids=true | all-gather | bytes 983040 | tf_op jit(solution)/shard_map/all_gather | solution.py:16
  52.1 4.9 %fusion.23 = bf16[256,2048]{1,0:T(8,128)(2,1)S(1)} fusion(bf16[256,1536]{1,0:T(8,128)(2,1)S(1)} %all_gather.12, bf16[1,1536,2048]{2,1,0:T(8,128)(2,1)} %param.11), kind=kOutput, calls=%fused_computation.24 | convolution fusion | flops 1611137024 | bytes 8126464 | tf_op jit(solution)/shard_map/dot_general | solution.py:81
  57.1 1.9 fusion.20
  59.0 1.5 pad_maximum_fusion
  60.6 0.0 reduce-scatter.9.cloned.1.call-start
  60.7 0.3 convolution_convert_fusion
  61.0 4.0 %copy.75 = bf16[2,8,6144]{1,0,2:T(2,128)(2,1)S(1)} copy(bf16[2,8,6144]{2,1,0:T(8,128)(2,1)S(1)} %convolution_convert_fusion) | data formatting | bytes 393216 | tf_op jit(solution)/shard_map/convert_element_type | solution.py:100
  65.0 3.4 %reshape.102 = bf16[4,2,12288]{2,1,0:T(2,128)(2,1)S(1)} reshape(bf16[6144,2,8]{2,1,0:T(2,128)(2,1)S(1)} %bitcast.90) | data formatting | bytes 393216
  68.4 16.1 %all_to_all.94 = bf16[4,2,12288]{2,1,0:T(2,128)(2,1)S(1)} all-to-all(bf16[4,2,12288]{2,1,0:T(2,128)(2,1)S(1)} %reshape.102), channel_id=1, replica_groups=mesh['dp'=4,'expert'=2,'tensor'=4] {'dp'}, dimensions={0} | all-to-all | bytes 393216 | tf_op jit(solution)/shard_map/all_to_all | solution.py:9
  84.5 3.7 %reshape.103 = bf16[6144,2,8]{2,1,0:T(2,128)(2,1)S(1)} reshape(bf16[4,2,12288]{2,1,0:T(2,128)(2,1)S(1)} %all_to_all.94) | data formatting | bytes 393216
  88.2 2.0 copy.81
  90.3 7.2 %all_to_all.95 = bf16[2,32,1536]{2,1,0:T(8,128)(2,1)S(1)} all-to-all(bf16[2,32,1536]{2,1,0:T(8,128)(2,1)S(1)} %bitcast.97), channel_id=1, replica_groups=mesh['dp'=4,'expert'=2,'tensor'=4] {'expert'}, dimensions={0} | all-to-all | bytes 393216 | tf_op jit(solution)/shard_map/all_to_all | solution.py:8
  97.5 8.5 %all_gather.14 = bf16[256,1536]{1,0:T(8,128)(2,1)S(1)} all-gather(bf16[64,1536]{1,0:T(8,128)(2,1)S(1)} %bitcast.99), channel_id=1, replica_groups=mesh['dp'=4,'expert'=2,'tensor'=4] {'tensor'}, dimensions={0}, use_global_device_ids=true | all-gather | bytes 983040 | tf_op jit(solution)/shard_map/all_gather | solution.py:16
  106.0 5.6 %fusion.29 = bf16[256,2048]{1,0:T(8,128)(2,1)} fusion(bf16[256,1536]{1,0:T(8,128)(2,1)S(1)} %all_gather.14, bf16[1,2048,1536]{2,1,0:T(8,128)(2,1)} %param.12), kind=kOutput, calls=%fused_computation.26 | convolution fusion | flops 1611137024 | bytes 8126464 | tf_op jit(solution)/shard_map/dot_general | solution.py:104
  111.6 0.0 all-gather.3.cloned.1.call-start
  111.7 1.1 convert_element_type.76
  112.8 23.8 %reduce-scatter.9.cloned.1.call-done = bf16[64,2048]{1,0:T(8,128)(2,1)} async-done(((bf16[256,2048]{1,0:T(8,128)(2,1)}), bf16[64,2048]{1,0:T(8,128)(2,1)}) %reduce-scatter.9.cloned.1.call-update) | async-done | bytes 262160 | tf_op jit(solution)/shard_map/reduce_scatter | solution.py:20
  136.6 2.0 fusion.38
  138.6 0.0 all-gather.5.cloned.1.call-start
  138.6 0.8 pad_maximum_fusion.1
  139.5 0.0 reduce-scatter.7.cloned.1.call-start
  139.5 25.8 %all-gather.3.cloned.1.call-done = bf16[256,2048]{1,0:T(8,128)(2,1)} async-done(((bf16[64,2048]{1,0:T(8,128)(2,1)}), bf16[256,2048]{1,0:T(8,128)(2,1)}) %all-gather.3.cloned.1.call-update) | async-done | bytes 1048592 | tf_op jit(solution)/shard_map/all_gather | solution.py:31
  165.3 5.8 %fusion.26 = bf16[256,1536]{1,0:T(8,128)(2,1)} fusion(bf16[256,2048]{1,0:T(8,128)(2,1)} %all-gather.3.cloned.1.call-done, bf16[1,2048,1536]{2,1,0:T(8,128)(2,1)} %param.12), kind=kOutput, calls=%fused_computation.25 | convolution fusion | flops 1611005952 | bytes 8126464 | tf_op jit(solution)/shard_map/dot_general | solution.py:91
  171.1 0.0 reduce-scatter.11.cloned.1.call-start
  171.2 41.6 %all-gather.5.cloned.1.call-done = bf16[256,4096]{1,0:T(8,128)(2,1)} async-done(((bf16[64,4096]{1,0:T(8,128)(2,1)}), bf16[256,4096]{1,0:T(8,128)(2,1)}) %all-gather.5.cloned.1.call-update) | async-done | bytes 2097168 | tf_op jit(solution)/shard_map/all_gather | solution.py:31
  212.8 5.1 %fusion.6 = f32[256,1536]{1,0:T(8,128)S(1)} fusion(bf16[1,1536,2048]{2,1,0:T(8,128)(2,1)} %param.11, bf16[256,4096]{1,0:T(8,128)(2,1)} %all-gather.5.cloned.1.call-done), kind=kOutput, calls=%fused_computation.13 | convolution fusion | flops 1610612736 | bytes 8912896 | tf_op jit(solution)/shard_map/dot_general | solution.py:127
  217.9 5.7 %fusion.17 = bf16[256,1536]{1,0:T(8,128)(2,1)} fusion(f32[256,1536]{1,0:T(8,128)S(1)} %fusion.6, bf16[1,1536,2048]{2,1,0:T(8,128)(2,1)} %param.10, bf16[256,4096]{1,0:T(8,128)(2,1)S(1)} %copy-done.4), kind=kOutput, calls=%fused_computation.22 | convolution fusion | flops 1611399168 | bytes 9699328 | tf_op jit(solution)/shard_map/dot_general | solution.py:124
  223.7 14.1 %reduce-scatter.7.cloned.1.call-done = bf16[64,1536]{1,0:T(8,128)(2,1)} async-done(((bf16[256,1536]{1,0:T(8,128)(2,1)}), bf16[64,1536]{1,0:T(8,128)(2,1)}) %reduce-scatter.7.cloned.1.call-update) | async-done | bytes 196624 | tf_op jit(solution)/shard_map/reduce_scatter | solution.py:37
  237.7 1.8 copy.73
  239.6 4.6 %all-to-all-start.2 = ((bf16[2,32,1536]{2,0,1:T(2,128)(2,1)}), bf16[2,32,1536]{2,0,1:T(2,128)(2,1)S(1)}, u32[]{:S(2)}, u32[]{:S(2)}) async-start(bf16[2,32,1536]{2,0,1:T(2,128)(2,1)} %copy.73), calls=%async_computation.4 | async-start | bytes 393216 | tf_op jit(solution)/shard_map/all_to_all | solution.py:42
  244.1 6.6 %convolution_bitcast_fusion = f32[1,2048,1536]{2,1,0:T(8,128)} fusion(bf16[256,2048]{1,0:T(8,128)(2,1)S(1)} %copy-done.5, bf16[256,1536]{1,0:T(8,128)(2,1)S(1)} %all_gather.14), kind=kOutput, calls=%fused_computation | convolution fusion | flops 1610612736 | bytes 14417920 | tf_op jit(solution)/shard_map/dot_general | solution.py:115
  250.8 13.4 %reduce-scatter.11.cloned.1.call-done = bf16[64,1536]{1,0:T(8,128)(2,1)} async-done(((bf16[256,1536]{1,0:T(8,128)(2,1)}), bf16[64,1536]{1,0:T(8,128)(2,1)}) %reduce-scatter.11.cloned.1.call-update) | async-done | bytes 196624 | tf_op jit(solution)/shard_map/reduce_scatter | solution.py:37
  264.2 1.8 copy.78
  266.0 4.6 %all-to-all-start.6 = ((bf16[2,32,1536]{2,0,1:T(2,128)(2,1)}), bf16[2,32,1536]{2,0,1:T(2,128)(2,1)S(1)}, u32[]{:S(2)}, u32[]{:S(2)}) async-start(bf16[2,32,1536]{2,0,1:T(2,128)(2,1)} %copy.78), calls=%async_computation.10 | async-start | bytes 393216 | tf_op jit(solution)/shard_map/all_to_all | solution.py:42
  270.6 7.8 %convolution_bitcast_fusion.2 = f32[1,1536,2048]{2,1,0:T(8,128)} fusion(bf16[256,1536]{1,0:T(8,128)(2,1)S(1)} %copy-done.3, bf16[256,4096]{1,0:T(8,128)(2,1)} %all-gather.5.cloned.1.call-done), kind=kOutput, calls=%fused_computation.2 | convolution fusion | flops 1610612736 | bytes 14417920 | tf_op jit(solution)/shard_map/dot_general | solution.py:118
  278.4 0.7 copy.74
  279.1 3.4 %all-to-all-start.3 = ((bf16[2,8,6144]{2,1,0:T(8,128)(2,1)}), bf16[2,8,6144]{2,1,0:T(8,128)(2,1)S(1)}, u32[]{:S(2)}, u32[]{:S(2)}) async-start(bf16[2,8,6144]{2,1,0:T(8,128)(2,1)} %bitcast.17), calls=%async_computation.5 | async-start | bytes 393216 | tf_op jit(solution)/shard_map/all_to_all | solution.py:41
  282.6 7.9 %convolution_bitcast_fusion.1 = f32[1,1536,2048]{2,1,0:T(8,128)} fusion(bf16[256,1536]{1,0:T(8,128)(2,1)S(1)} %copy-done.3, bf16[256,4096]{1,0:T(8,128)(2,1)} %all-gather.5.cloned.1.call-done), kind=kOutput, calls=%fused_computation.1 | convolution fusion | flops 1610612736 | bytes 14417920 | tf_op jit(solution)/shard_map/dot_general | solution.py:121
  290.4 0.7 copy.79
  291.1 3.4 %all-to-all-start.7 = ((bf16[2,8,6144]{2,1,0:T(8,128)(2,1)}), bf16[2,8,6144]{2,1,0:T(8,128)(2,1)S(1)}, u32[]{:S(2)}, u32[]{:S(2)}) async-start(bf16[2,8,6144]{2,1,0:T(8,128)(2,1)} %bitcast.26), calls=%async_computation.11 | async-start | bytes 393216 | tf_op jit(solution)/shard_map/all_to_all | solution.py:41
  294.6 1.0 fusion
  295.6 3.8 %all-to-all-done.7 = bf16[2,8,6144]{2,1,0:T(8,128)(2,1)S(1)} async-done(((bf16[2,8,6144]{2,1,0:T(8,128)(2,1)}), bf16[2,8,6144]{2,1,0:T(8,128)(2,1)S(1)}, u32[]{:S(2)}, u32[]{:S(2)}) %all-to-all-start.7) | async-done | bytes 196640 | tf_op jit(solution)/shard_map/all_to_all | solution.py:41
  299.4 1.0 fusion.1
  (39 shorter events, 0.3 us)
Async XLA Ops:
  7.2 1.8 copy-start
  7.2 104.5 %reduce-scatter.5.cloned.1.call-start = ((), (), s32[]{:S(2)}) async-start(), calls=%async_computation.12 | async-start | bytes 2621440 | tf_op jit(solution)/shard_map/reduce_scatter | solution.py:20
  43.4 13.7 %slice-start = ((s8[6291456]{0:T(1024)(128)(4,1)}), s8[4194304]{0:T(1024)(128)(4,1)S(1)}, s32[]{:S(2)}) async-start(s8[6291456]{0:T(1024)(128)(4,1)} %bitcast.112), calls=%async_computation.18 | async-start | bytes 8388608
  52.1 4.9 %copy-start.2 = (bf16[256,1536]{1,0:T(8,128)(2,1)}, bf16[256,1536]{1,0:T(8,128)(2,1)S(1)}, u32[]{:S(2)}) copy-start(bf16[256,1536]{1,0:T(8,128)(2,1)S(1)} %all_gather.12) | copy-start | bytes 2359300
  52.1 4.9 %slice-start.1 = ((s8[6291456]{0:T(1024)(128)(4,1)}), s8[2097152]{0:T(1024)(128)(4,1)S(1)}, s32[]{:S(2)}) async-start(s8[6291456]{0:T(1024)(128)(4,1)} %bitcast.112), calls=%async_computation.19 | async-start | bytes 4194304
  59.0 1.7 copy-start.6
  59.0 1.7 copy-start.7
  59.0 1.7 copy-start.8
  60.6 76.0 %reduce-scatter.9.cloned.1.call-start = ((), (), s32[]{:S(2)}) async-start(), calls=%async_computation.15 | async-start | bytes 1310720 | tf_op jit(solution)/shard_map/reduce_scatter | solution.py:20
  111.6 53.7 %all-gather.3.cloned.1.call-start = ((), (), s32[]{:S(2)}) async-start(), calls=%async_computation.13 | async-start | bytes 1310720 | tf_op jit(solution)/shard_map/all_gather | solution.py:31
  138.6 74.2 %all-gather.5.cloned.1.call-start = ((), (), s32[]{:S(2)}) async-start(), calls=%async_computation.16 | async-start | bytes 2621440 | tf_op jit(solution)/shard_map/all_gather | solution.py:31
  139.5 98.3 %reduce-scatter.7.cloned.1.call-start = ((), (), s32[]{:S(2)}) async-start(), calls=%async_computation.14 | async-start | bytes 983040 | tf_op jit(solution)/shard_map/reduce_scatter | solution.py:37
  171.1 93.0 %reduce-scatter.11.cloned.1.call-start = ((), (), s32[]{:S(2)}) async-start(), calls=%async_computation.17 | async-start | bytes 983040 | tf_op jit(solution)/shard_map/reduce_scatter | solution.py:37
  212.8 5.1 %copy-start.4 = (bf16[256,4096]{1,0:T(8,128)(2,1)S(1)}, bf16[256,4096]{1,0:T(8,128)(2,1)}, u32[]{:S(2)}) copy-start(bf16[256,4096]{1,0:T(8,128)(2,1)} %all-gather.5.cloned.1.call-done) | copy-start | bytes 6291460
  217.9 26.3 %copy-start.5 = (bf16[256,2048]{1,0:T(8,128)(2,1)S(1)}, bf16[256,2048]{1,0:T(8,128)(2,1)}, u32[]{:S(2)}) copy-start(bf16[256,2048]{1,0:T(8,128)(2,1)} %all-gather.3.cloned.1.call-done) | copy-start | bytes 3145732
  239.6 26.4 %all-to-all-start.2 = ((bf16[2,32,1536]{2,0,1:T(2,128)(2,1)}), bf16[2,32,1536]{2,0,1:T(2,128)(2,1)S(1)}, u32[]{:S(2)}, u32[]{:S(2)}) async-start(bf16[2,32,1536]{2,0,1:T(2,128)(2,1)} %copy.73), calls=%async_computation.4 | async-start | bytes 393216 | tf_op jit(solution)/shard_map/all_to_all | solution.py:42
  244.1 26.4 %copy-start.3 = (bf16[256,1536]{1,0:T(8,128)(2,1)S(1)}, bf16[256,1536]{1,0:T(8,128)(2,1)}, u32[]{:S(2)}) copy-start(bf16[256,1536]{1,0:T(8,128)(2,1)} %copy-done.2) | copy-start | bytes 2359300
  266.0 13.1 %all-to-all-start.6 = ((bf16[2,32,1536]{2,0,1:T(2,128)(2,1)}), bf16[2,32,1536]{2,0,1:T(2,128)(2,1)S(1)}, u32[]{:S(2)}, u32[]{:S(2)}) async-start(bf16[2,32,1536]{2,0,1:T(2,128)(2,1)} %copy.78), calls=%async_computation.10 | async-start | bytes 393216 | tf_op jit(solution)/shard_map/all_to_all | solution.py:42
  279.1 12.0 %all-to-all-start.3 = ((bf16[2,8,6144]{2,1,0:T(8,128)(2,1)}), bf16[2,8,6144]{2,1,0:T(8,128)(2,1)S(1)}, u32[]{:S(2)}, u32[]{:S(2)}) async-start(bf16[2,8,6144]{2,1,0:T(8,128)(2,1)} %bitcast.17), calls=%async_computation.5 | async-start | bytes 393216 | tf_op jit(solution)/shard_map/all_to_all | solution.py:41
  282.6 17.9 %copy-start.1 = (bf16[16,6144]{1,0:T(8,128)(2,1)S(1)}, bf16[16,6144]{1,0:T(8,128)(2,1)}, u32[]{:S(2)}) copy-start(bf16[16,6144]{1,0:T(8,128)(2,1)} %param.7) | copy-start | bytes 589828
  291.1 8.2 %all-to-all-start.7 = ((bf16[2,8,6144]{2,1,0:T(8,128)(2,1)}), bf16[2,8,6144]{2,1,0:T(8,128)(2,1)S(1)}, u32[]{:S(2)}, u32[]{:S(2)}) async-start(bf16[2,8,6144]{2,1,0:T(8,128)(2,1)} %bitcast.26), calls=%async_computation.11 | async-start | bytes 393216 | tf_op jit(solution)/shard_map/all_to_all | solution.py:41
Sparse Core Ops, SparseCore 0:
  60.7 44.2 reduce-scatter.4
  111.7 24.7 reduce-scatter.8
  138.7 26.5 all-gather.2
  167.3 45.4 all-gather.4
  215.7 21.9 reduce-scatter.6
  240.9 23.2 reduce-scatter.10
where the time goes:
time: 308 us; the launch traced here: 307 us
  waiting for transfers between devices  123 us (40%)
  blocking collectives  61.6 us (20%)
  matrix products  53.9 us (18%)
  local copies, waits for them, and re-layouts  32 us (10%)
  starting transfers between devices  16.3 us (5%)
  between operations  14.4 us (5%)
  other arithmetic  6.59 us (2%)
    all_gather x2, waiting for transfers between devices, gather_rows(): return lax.all_gather(values, 'dp', axis=0, tiled=True)  67.4 us
    all_to_all x2, blocking collectives, spread(): lax.all_to_all(send_rows, 'dp', split_axis=2, concat_axis=1, tiled=True)  29.7 us
    reduce_scatter x2, waiting for transfers between devices, collect(): lax.psum_scatter(partial_rows.astype(jnp.bfloat16), 'tensor', scatter_dim...  27.5 us
    reduce_scatter x2, waiting for transfers between devices, width_sums(): lax.psum_scatter(term_fn(jnp.int32(0), total_rows // lax.axis_size('dp')...  23.8 us
    all_gather x2, blocking collectives, spread(): return lax.all_gather(flat, 'tensor', axis=0, tiled=True)  17.3 us
    all_to_all x2, blocking collectives, spread(): lax.all_to_all(lax.all_to_all(send_rows, 'dp', split_axis=2, concat_axis=...  14.6 us
    unnamed x26, local copies, waits for them, and re-layouts  14.2 us
    all_to_all x2, starting transfers between devices, collect(): lax.all_to_all(local, 'dp', split_axis=1, concat_axis=2, tiled=True)  9.18 us
  transfers between devices with their start and end apart: 10, of which 6 were waited for; matrix products, arithmetic and copies ran while one was open for 21% of the time, Pallas kernels for 0%

commit v1 on v0

--- a/solution.py
+++ b/solution.py
@@ -1,19 +1,132 @@
+import functools
+
 import jax
 import jax.numpy as jnp
 from jax import lax
+from jax.experimental import pallas as pl
+from jax.experimental.pallas import tpu as pltpu
 from jax.sharding import PartitionSpec as P
 
-
-def spread(send_rows):
-    moved = lax.all_to_all(
-        lax.all_to_all(send_rows, "dp", split_axis=2, concat_axis=1, tiled=True),
-        "expert",
-        split_axis=0,
-        concat_axis=0,
-        tiled=True,
-    )
-    flat = moved.reshape(-1, moved.shape[2])
-    return lax.all_gather(flat, "tensor", axis=0, tiled=True)
+MESH = pl.DeviceIdType.MESH
+
+
+def remote(src, dst, send_sem, recv_sem, device):
+    return pltpu.make_async_remote_copy(
+        src_ref=src,
+        dst_ref=dst,
+        send_sem=send_sem,
+        recv_sem=recv_sem,
+        device_id=device,
+        device_id_type=MESH,
+    )
+
+
+def dispatch_kernel(n_dp, n_exp, n_t, send_ref, out_ref, s1, r1, s2, r2, s3, own_sem):
+    d, e, t = lax.axis_index("dp"), lax.axis_index("expert"), lax.axis_index("tensor")
+    width = out_ref.shape[3]
+    core = lax.rem(t, 2)
+    mate = t + 1 - 2 * core
+    offsets = [(dd, de) for dd in range(n_dp) for de in range(n_exp)]
+    offsets = offsets[1:] + offsets[:1]
+    peers = [lax.rem(t + 2 * k, n_t) for k in range(1, n_t // 2)]
+
+    def at(dp, expert, tensor):
+        return (dp, expert, tensor)
+
+    barrier = pltpu.get_barrier_semaphore()
+    for dd, de in offsets[:-1]:
+        pl.semaphore_signal(
+            barrier,
+            inc=1,
+            device_id=at(lax.rem(d + dd, n_dp), lax.rem(e + de, n_exp), t),
+            device_id_type=MESH,
+        )
+    for peer in peers + [mate]:
+        pl.semaphore_signal(barrier, inc=1, device_id=at(d, e, peer), device_id_type=MESH)
+    pl.semaphore_wait(barrier, len(offsets) - 1 + len(peers) + 1)
+
+    mine = e * n_dp + d
+    first = []
+    for k, (dd, de) in enumerate(offsets):
+        dp_to, exp_to = lax.rem(d + dd, n_dp), lax.rem(e + de, n_exp)
+        block = send_ref.at[exp_to, :, pl.ds(pl.multiple_of(dp_to * width, 128), width)]
+        if k == len(offsets) - 1:
+            own = pltpu.make_async_copy(block, out_ref.at[t, mine], own_sem)
+            own.start()
+        else:
+            copy = remote(block, out_ref.at[t, mine], s1.at[k], r1.at[k], at(dp_to, exp_to, t))
+            copy.start()
+            first.append(copy)
+    second = []
+    order = [len(offsets) - 1] + list(range(len(offsets) - 1))
+    for k in order:
+        dd, de = offsets[k]
+        source = lax.rem(e + n_exp - de, n_exp) * n_dp + lax.rem(d + n_dp - dd, n_dp)
+        if k == len(offsets) - 1:
+            own.wait()
+        else:
+            remote(
+                out_ref.at[t, source], out_ref.at[t, source], s1.at[k], r1.at[k], at(d, e, mate)
+            ).wait_recv()
+        for j, peer in enumerate(peers + [mate]):
+            copy = remote(
+                out_ref.at[t, source],
+                out_ref.at[t, source],
+                s2.at[j, k],
+                r2.at[j, k],
+                at(d, e, peer),
+            )
+            copy.start()
+            second.append(copy)
+    third = []
+    for k in order:
+        dd, de = offsets[k]
+        source = lax.rem(e + n_exp - de, n_exp) * n_dp + lax.rem(d + n_dp - dd, n_dp)
+        for j in range(len(peers)):
+            origin = lax.rem(t + n_t - 2 * (j + 1), n_t)
+            block = out_ref.at[origin, source]
+            remote(block, block, s2.at[j, k], r2.at[j, k], at(d, e, mate)).wait_recv()
+            copy = remote(block, block, s3.at[j, k], r2.at[len(peers) + 1 + j, k], at(d, e, mate))
+            copy.start()
+            third.append(copy)
+    for k in order:
+        dd, de = offsets[k]
+        source = lax.rem(e + n_exp - de, n_exp) * n_dp + lax.rem(d + n_dp - dd, n_dp)
+        block = out_ref.at[mate, source]
+        remote(
+            block, block, s2.at[len(peers), k], r2.at[len(peers), k], at(d, e, mate)
+        ).wait_recv()
+        for j in range(len(peers)):
+            block = out_ref.at[lax.rem(mate + n_t - 2 * (j + 1), n_t), source]
+            remote(
+                block, block, s3.at[j, k], r2.at[len(peers) + 1 + j, k], at(d, e, mate)
+            ).wait_recv()
+    for copy in first + second + third:
+        copy.wait_send()
+
+
+def dispatch(send, n_dp, n_exp, n_t):
+    rows, model = send.shape[1], send.shape[2]
+    sources = n_dp * n_exp
+    peers = n_t // 2 - 1
+    return pl.pallas_call(
+        functools.partial(dispatch_kernel, n_dp, n_exp, n_t),
+        out_shape=jax.ShapeDtypeStruct((n_t, sources, rows, model // n_dp), jnp.bfloat16),
+        in_specs=[pl.BlockSpec(memory_space=pltpu.VMEM)],
+        out_specs=pl.BlockSpec(memory_space=pltpu.VMEM),
+        scratch_shapes=[
+            pltpu.SemaphoreType.DMA((sources,)),
+            pltpu.SemaphoreType.DMA((sources,)),
+            pltpu.SemaphoreType.DMA((peers + 1, sources)),
+            pltpu.SemaphoreType.DMA((2 * peers + 1, sources)),
+            pltpu.SemaphoreType.DMA((peers, sources)),
+            pltpu.SemaphoreType.DMA,
+        ],
+        compiler_params=pltpu.CompilerParams(
+            collective_id=0, has_side_effects=True, vmem_limit_bytes=32 * 1024 * 1024
+        ),
+        name="dispatch",
+    )(send)
 
 
 def width_sums(term_fn, total_rows):
@@ -73,7 +186,15 @@
     send_rows = jnp.einsum(
         "wct,td->wcd", selector_bf, tokens, preferred_element_type=jnp.float32
     ).astype(jnp.bfloat16)
-    panel_rows = spread(send_rows)
+    scaled = (weights[:, :, None] * grad_out.astype(jnp.float32)[None]).astype(jnp.bfloat16)
+    send_grads = jnp.einsum(
+        "wct,wtd->wcd", selector_bf, scaled, preferred_element_type=jnp.float32
+    ).astype(jnp.bfloat16)
+    n_dp, n_t = lax.axis_size("dp"), lax.axis_size("tensor")
+    panels = dispatch(jnp.concatenate([send_rows, send_grads], axis=1), n_dp, n_exp, n_t)
+    quarter = panels.shape[3]
+    panel_rows = panels[:, :, :cap].reshape(-1, quarter)
+    grad_panels = panels[:, :, cap:].reshape(-1, quarter)
     total_rows = panel_rows.shape[0]
 
     def forward_term(start, count):
@@ -94,12 +215,6 @@
     mixed = jnp.einsum(
         "wct,wcd->td", weighted, out_home.astype(jnp.float32), precision=lax.Precision.HIGHEST
     ).astype(jnp.bfloat16)
-    scaled = (weights[:, :, None] * grad_out.astype(jnp.float32)[None]).astype(jnp.bfloat16)
-    send_grads = jnp.einsum(
-        "wct,wtd->wcd", selector_bf, scaled, preferred_element_type=jnp.float32
-    ).astype(jnp.bfloat16)
-    grad_panels = spread(send_grads)
-
     def backward_term(start, count):
         return lax.dot_general(
             grad_panels, down_mat, (((1,), (1,)), ((), ())), preferred_element_type=jnp.float32

time: 308 us -> 283 us (0.919)
  blocking collectives: 61.6 us -> 0 us
  waiting for transfers between devices: 123 us -> 166 us
  local copies, waits for them, and re-layouts: 32 us -> 6.77 us
  Pallas kernels: 0 us -> 20.2 us
  matrix products: 53.9 us -> 50.7 us
    all_to_all x4 -> x0, blocking collectives: 44.3 us -> none  [the longest x2 29.7 us: spread(): lax.all_to_all(send_rows, 'dp', split_axis=2, concat_axis=1, tiled=True)]
    reduce_scatter x2, waiting for transfers between devices: 23.8 us -> 67.4 us  [width_sums(): lax.psum_scatter(term_fn(jnp.int32(0), total_rows // lax.axis_size('dp')...]
    pallas_call x0 -> x1, Pallas kernels: none -> 20.2 us  [dispatch(): pl.pallas_call(functools.partial(dispatch_kernel, n_dp, n_exp, n_t), out_...]
    all_gather x2 -> x0, blocking collectives: 17.3 us -> none  [spread(): return lax.all_gather(flat, 'tensor', axis=0, tiled=True)]
    unnamed x26 -> x14, local copies, waits for them, and re-layouts: 14.2 us -> 0.97 us
    convert_element_type x2 -> x0, local copies, waits for them, and re-layouts: 8.04 us -> none  [the longest x1 4.02 us: body(): send_rows = jnp.einsum('wct,td->wcd', selector_bf, tokens, preferred_elem...]
    all_to_all x4 -> x0, local copies, waits for them, and re-layouts: 4.1 us -> none  [spread(): lax.all_to_all(send_rows, 'dp', split_axis=2, concat_axis=1, tiled=True)]
    dot_general x1, matrix products: 4.91 us -> 1.79 us  [forward_term(): up_part = jnp.dot(panel_rows, up_mat, preferred_element_type=jnp.float32)]
  transfers between devices with their start and end apart: 10 -> 10, of which waited for: 6 -> 7; matrix products, arithmetic and copies ran while one was open for 21% -> 19% of each run, Pallas kernels for 0% -> 0%
where the time goes in v1:
time: 283 us
  waiting for transfers between devices  166 us (59%)
  matrix products  50.7 us (18%)
  Pallas kernels  20.2 us (7%)
  starting transfers between devices  16.3 us (6%)
  between operations  14.3 us (5%)
  other arithmetic  8.23 us (3%)
  local copies, waits for them, and re-layouts  6.77 us (2%)
    all_gather x2, waiting for transfers between devices, gather_rows(): return lax.all_gather(values, 'dp', axis=0, tiled=True)  67.4 us
    reduce_scatter x2, waiting for transfers between devices, width_sums(): lax.psum_scatter(term_fn(jnp.int32(0), total_rows // lax.axis_size('dp')...  67.4 us
    reduce_scatter x2, waiting for transfers between devices, collect(): lax.psum_scatter(partial_rows.astype(jnp.bfloat16), 'tensor', scatter_dim...  27.5 us
    pallas_call x1, Pallas kernels, dispatch(): pl.pallas_call(functools.partial(dispatch_kernel, n_dp, n_exp, n_t), out_...  20.2 us
    all_to_all x2, starting transfers between devices, collect(): lax.all_to_all(local, 'dp', split_axis=1, concat_axis=2, tiled=True)  9.2 us
    dot_general x1, matrix products, body(): lax.dot_general(panel_rows, dup_all, (((0,), (0,)), ((), ())), preferred_...  7.87 us
    dot_general x1, matrix products, body(): lax.dot_general(panel_rows, dgate_all, (((0,), (0,)), ((), ())), preferre...  7.83 us
    all_to_all x2, starting transfers between devices, collect(): lax.all_to_all(lax.all_to_all(local, 'dp', split_axis=1, concat_axis=2, t...  6.86 us
  transfers between devices with their start and end apart: 10, of which 7 were waited for; matrix products, arithmetic and copies ran while one was open for 19% of the time, Pallas kernels for 0%

profile of v1, /device:TPU:0, one launch (start us, length us, event | category | flops | bytes accessed | tf_op | source)
XLA Modules:
  0.0 282.7 jit_solution(12586279260901180774)
XLA Ops:
  7.2 0.0 copy-start
  7.2 0.0 reduce-scatter.5.cloned.1.call-start
  7.2 1.0 convert_element_type.76
  8.2 0.7 broadcast_compare_fusion.1
  8.9 0.7 multiply_reduce_fusion.1
  9.6 0.1 copy.37
  9.7 0.1 reshape.97
  9.8 0.1 reduce-window.9
  9.8 0.1 add_reduce_fusion
  9.9 0.1 sub.16
  10.0 0.1 copy.39
  10.1 0.1 copy.34
  10.2 0.1 reshape.96
  10.3 0.1 reduce-window.6
  10.3 0.1 add_reduce_fusion.1
  10.5 0.1 sub.14
  10.5 0.1 copy.36
  10.7 0.2 convolution_convert_fusion.1
  10.9 0.3 convolution_convert_fusion
  11.2 20.2 %dispatch.1 = bf16[4,8,16,1536]{3,2,1,0:T(8,128)(2,1)S(1)} custom-call(bf16[2,16,6144]{2,1,0:T(8,128)(2,1)S(1)} %pad_maximum_fusion.2.send_ref), custom_call_target="tpu_custom_call" | custom-call | tf_op jit(solution)/shard_map/dispatch/pallas_call | solution.py:112
  31.4 0.1 fusion.55
  31.6 1.8 fusion.23
  33.3 0.2 slice-done
  33.6 0.7 slice-done.1
  34.3 1.9 fusion.20
  36.2 1.5 pad_maximum_fusion
  37.7 0.0 reduce-scatter.5.cloned.1.call-update
  37.8 0.0 reduce-scatter.9.cloned.1.call-start
  37.8 5.6 %fusion.29 = bf16[256,2048]{1,0:T(8,128)(2,1)} fusion(bf16[256,1536]{1,0:T(8,128)(2,1)S(1)} %bitcast.78, bf16[1,2048,1536]{2,1,0:T(8,128)(2,1)} %param.12), kind=kOutput, calls=%fused_computation.26 | convolution fusion | flops 1611137024 | bytes 8126464 | tf_op jit(solution)/shard_map/dot_general | solution.py:219
  43.4 0.0 reduce-scatter.9.cloned.1.call-update
  43.4 0.0 all-gather.3.cloned.1.call-start
  43.5 39.0 %reduce-scatter.5.cloned.1.call-done = bf16[64,4096]{1,0:T(8,128)(2,1)} async-done(((bf16[256,4096]{1,0:T(8,128)(2,1)}), bf16[64,4096]{1,0:T(8,128)(2,1)}) %reduce-scatter.5.cloned.1.call-update) | async-done | bytes 524304 | tf_op jit(solution)/shard_map/reduce_scatter | solution.py:133
  82.5 1.1 convert_element_type.79
  83.6 28.4 %reduce-scatter.9.cloned.1.call-done = bf16[64,2048]{1,0:T(8,128)(2,1)} async-done(((bf16[256,2048]{1,0:T(8,128)(2,1)}), bf16[64,2048]{1,0:T(8,128)(2,1)}) %reduce-scatter.9.cloned.1.call-update) | async-done | bytes 262160 | tf_op jit(solution)/shard_map/reduce_scatter | solution.py:133
  112.0 2.0 fusion.38
  113.9 0.0 all-gather.3.cloned.1.call-update
  113.9 0.0 all-gather.5.cloned.1.call-start
  114.0 0.8 pad_maximum_fusion.1
  114.8 0.0 all-gather.5.cloned.1.call-update
  114.9 0.0 reduce-scatter.7.cloned.1.call-start
  114.9 25.8 %all-gather.3.cloned.1.call-done = bf16[256,2048]{1,0:T(8,128)(2,1)} async-done(((bf16[64,2048]{1,0:T(8,128)(2,1)}), bf16[256,2048]{1,0:T(8,128)(2,1)}) %all-gather.3.cloned.1.call-update) | async-done | bytes 1048592 | tf_op jit(solution)/shard_map/all_gather | solution.py:144
  140.7 5.8 %fusion.26 = bf16[256,1536]{1,0:T(8,128)(2,1)} fusion(bf16[256,2048]{1,0:T(8,128)(2,1)} %all-gather.3.cloned.1.call-done, bf16[1,2048,1536]{2,1,0:T(8,128)(2,1)} %param.12), kind=kOutput, calls=%fused_computation.25 | convolution fusion | flops 1611005952 | bytes 8126464 | tf_op jit(solution)/shard_map/dot_general | solution.py:212
  146.5 0.0 reduce-scatter.7.cloned.1.call-update
  146.6 0.0 reduce-scatter.11.cloned.1.call-start
  146.6 41.6 %all-gather.5.cloned.1.call-done = bf16[256,4096]{1,0:T(8,128)(2,1)} async-done(((bf16[64,4096]{1,0:T(8,128)(2,1)}), bf16[256,4096]{1,0:T(8,128)(2,1)}) %all-gather.5.cloned.1.call-update) | async-done | bytes 2097168 | tf_op jit(solution)/shard_map/all_gather | solution.py:144
  188.2 5.1 %fusion.6 = f32[256,1536]{1,0:T(8,128)S(1)} fusion(bf16[1,1536,2048]{2,1,0:T(8,128)(2,1)} %param.11, bf16[256,4096]{1,0:T(8,128)(2,1)} %all-gather.5.cloned.1.call-done), kind=kOutput, calls=%fused_computation.13 | convolution fusion | flops 1610612736 | bytes 8912896 | tf_op jit(solution)/shard_map/dot_general | solution.py:242
  193.3 5.7 %fusion.17 = bf16[256,1536]{1,0:T(8,128)(2,1)} fusion(f32[256,1536]{1,0:T(8,128)S(1)} %fusion.6, bf16[1,1536,2048]{2,1,0:T(8,128)(2,1)} %param.10, bf16[256,4096]{1,0:T(8,128)(2,1)S(1)} %copy-done.2), kind=kOutput, calls=%fused_computation.22 | convolution fusion | flops 1611399168 | bytes 9699328 | tf_op jit(solution)/shard_map/dot_general | solution.py:239
  199.0 0.0 reduce-scatter.11.cloned.1.call-update
  199.0 14.1 %reduce-scatter.7.cloned.1.call-done = bf16[64,1536]{1,0:T(8,128)(2,1)} async-done(((bf16[256,1536]{1,0:T(8,128)(2,1)}), bf16[64,1536]{1,0:T(8,128)(2,1)}) %reduce-scatter.7.cloned.1.call-update) | async-done | bytes 196624 | tf_op jit(solution)/shard_map/reduce_scatter | solution.py:150
  213.1 1.8 copy.40
  214.9 4.6 %all-to-all-start = ((bf16[2,32,1536]{2,0,1:T(2,128)(2,1)}), bf16[2,32,1536]{2,0,1:T(2,128)(2,1)S(1)}, u32[]{:S(2)}, u32[]{:S(2)}) async-start(bf16[2,32,1536]{2,0,1:T(2,128)(2,1)} %copy.40), calls=%async_computation.2 | async-start | bytes 393216 | tf_op jit(solution)/shard_map/all_to_all | solution.py:155
  219.6 6.6 %convolution_bitcast_fusion = f32[1,2048,1536]{2,1,0:T(8,128)} fusion(bf16[256,2048]{1,0:T(8,128)(2,1)S(1)} %copy-done.3, bf16[256,1536]{1,0:T(8,128)(2,1)S(1)} %bitcast.79), kind=kOutput, calls=%fused_computation | convolution fusion | flops 1610612736 | bytes 14417920 | tf_op jit(solution)/shard_map/dot_general | solution.py:230
  226.2 13.4 %reduce-scatter.11.cloned.1.call-done = bf16[64,1536]{1,0:T(8,128)(2,1)} async-done(((bf16[256,1536]{1,0:T(8,128)(2,1)}), bf16[64,1536]{1,0:T(8,128)(2,1)}) %reduce-scatter.11.cloned.1.call-update) | async-done | bytes 196624 | tf_op jit(solution)/shard_map/reduce_scatter | solution.py:150
  239.6 1.8 copy.42
  241.4 4.6 %all-to-all-start.2 = ((bf16[2,32,1536]{2,0,1:T(2,128)(2,1)}), bf16[2,32,1536]{2,0,1:T(2,128)(2,1)S(1)}, u32[]{:S(2)}, u32[]{:S(2)}) async-start(bf16[2,32,1536]{2,0,1:T(2,128)(2,1)} %copy.42), calls=%async_computation.6 | async-start | bytes 393216 | tf_op jit(solution)/shard_map/all_to_all | solution.py:155
  246.0 7.8 %convolution_bitcast_fusion.2 = f32[1,1536,2048]{2,1,0:T(8,128)} fusion(bf16[256,1536]{1,0:T(8,128)(2,1)S(1)} %bitcast.76, bf16[256,4096]{1,0:T(8,128)(2,1)} %all-gather.5.cloned.1.call-done), kind=kOutput, calls=%fused_computation.2 | convolution fusion | flops 1610612736 | bytes 14417920 | tf_op jit(solution)/shard_map/dot_general | solution.py:233
  253.8 0.7 copy.41
  254.5 3.4 %all-to-all-start.1 = ((bf16[2,8,6144]{2,1,0:T(8,128)(2,1)}), bf16[2,8,6144]{2,1,0:T(8,128)(2,1)S(1)}, u32[]{:S(2)}, u32[]{:S(2)}) async-start(bf16[2,8,6144]{2,1,0:T(8,128)(2,1)} %bitcast.14), calls=%async_computation.3 | async-start | bytes 393216 | tf_op jit(solution)/shard_map/all_to_all | solution.py:154
  258.0 7.9 %convolution_bitcast_fusion.1 = f32[1,1536,2048]{2,1,0:T(8,128)} fusion(bf16[256,1536]{1,0:T(8,128)(2,1)S(1)} %bitcast.77, bf16[256,4096]{1,0:T(8,128)(2,1)} %all-gather.5.cloned.1.call-done), kind=kOutput, calls=%fused_computation.1 | convolution fusion | flops 1610612736 | bytes 14417920 | tf_op jit(solution)/shard_map/dot_general | solution.py:236
  265.9 0.7 copy.43
  266.6 3.4 %all-to-all-start.3 = ((bf16[2,8,6144]{2,1,0:T(8,128)(2,1)}), bf16[2,8,6144]{2,1,0:T(8,128)(2,1)S(1)}, u32[]{:S(2)}, u32[]{:S(2)}) async-start(bf16[2,8,6144]{2,1,0:T(8,128)(2,1)} %bitcast.20), calls=%async_computation.7 | async-start | bytes 393216 | tf_op jit(solution)/shard_map/all_to_all | solution.py:154
  270.0 1.0 fusion
  271.0 3.8 %all-to-all-done.3 = bf16[2,8,6144]{2,1,0:T(8,128)(2,1)S(1)} async-done(((bf16[2,8,6144]{2,1,0:T(8,128)(2,1)}), bf16[2,8,6144]{2,1,0:T(8,128)(2,1)S(1)}, u32[]{:S(2)}, u32[]{:S(2)}) %all-to-all-start.3) | async-done | bytes 196640 | tf_op jit(solution)/shard_map/all_to_all | solution.py:154
  274.8 1.0 fusion.1
  (18 shorter events, 0.1 us)
Async XLA Ops:
  7.2 3.5 %copy-start = (bf16[16,6144]{1,0:T(8,128)(2,1)S(1)}, bf16[16,6144]{1,0:T(8,128)(2,1)}, u32[]{:S(2)}) copy-start(bf16[16,6144]{1,0:T(8,128)(2,1)} %param.7) | copy-start | bytes 589828
  7.2 75.3 %reduce-scatter.5.cloned.1.call-start = ((), (), s32[]{:S(2)}) async-start(), calls=%async_computation.8 | async-start | bytes 2621440 | tf_op jit(solution)/shard_map/reduce_scatter | solution.py:133
  10.6 20.9 %copy-start.4 = (bf16[1,1536,2048]{2,1,0:T(8,128)(2,1)S(1)}, bf16[1,1536,2048]{2,1,0:T(8,128)(2,1)}, u32[]{:S(2)}) copy-start(bf16[1,1536,2048]{2,1,0:T(8,128)(2,1)} %param.11) | copy-start | bytes 18874372
  31.4 2.2 slice-start
  31.5 2.7 slice-start.1
  37.8 74.2 %reduce-scatter.9.cloned.1.call-start = ((), (), s32[]{:S(2)}) async-start(), calls=%async_computation.11 | async-start | bytes 1310720 | tf_op jit(solution)/shard_map/reduce_scatter | solution.py:133
  43.4 97.3 %all-gather.3.cloned.1.call-start = ((), (), s32[]{:S(2)}) async-start(), calls=%async_computation.9 | async-start | bytes 1310720 | tf_op jit(solution)/shard_map/all_gather | solution.py:144
  113.9 74.2 %all-gather.5.cloned.1.call-start = ((), (), s32[]{:S(2)}) async-start(), calls=%async_computation.12 | async-start | bytes 2621440 | tf_op jit(solution)/shard_map/all_gather | solution.py:144
  114.9 98.3 %reduce-scatter.7.cloned.1.call-start = ((), (), s32[]{:S(2)}) async-start(), calls=%async_computation.10 | async-start | bytes 983040 | tf_op jit(solution)/shard_map/reduce_scatter | solution.py:150
  146.6 93.0 %reduce-scatter.11.cloned.1.call-start = ((), (), s32[]{:S(2)}) async-start(), calls=%async_computation.13 | async-start | bytes 983040 | tf_op jit(solution)/shard_map/reduce_scatter | solution.py:150
  188.2 5.1 %copy-start.2 = (bf16[256,4096]{1,0:T(8,128)(2,1)S(1)}, bf16[256,4096]{1,0:T(8,128)(2,1)}, u32[]{:S(2)}) copy-start(bf16[256,4096]{1,0:T(8,128)(2,1)} %all-gather.5.cloned.1.call-done) | copy-start | bytes 6291460
  193.3 26.3 %copy-start.3 = (bf16[256,2048]{1,0:T(8,128)(2,1)S(1)}, bf16[256,2048]{1,0:T(8,128)(2,1)}, u32[]{:S(2)}) copy-start(bf16[256,2048]{1,0:T(8,128)(2,1)} %all-gather.3.cloned.1.call-done) | copy-start | bytes 3145732
  214.9 26.5 %all-to-all-start = ((bf16[2,32,1536]{2,0,1:T(2,128)(2,1)}), bf16[2,32,1536]{2,0,1:T(2,128)(2,1)S(1)}, u32[]{:S(2)}, u32[]{:S(2)}) async-start(bf16[2,32,1536]{2,0,1:T(2,128)(2,1)} %copy.40), calls=%async_computation.2 | async-start | bytes 393216 | tf_op jit(solution)/shard_map/all_to_all | solution.py:155
  241.4 13.1 %all-to-all-start.2 = ((bf16[2,32,1536]{2,0,1:T(2,128)(2,1)}), bf16[2,32,1536]{2,0,1:T(2,128)(2,1)S(1)}, u32[]{:S(2)}, u32[]{:S(2)}) async-start(bf16[2,32,1536]{2,0,1:T(2,128)(2,1)} %copy.42), calls=%async_computation.6 | async-start | bytes 393216 | tf_op jit(solution)/shard_map/all_to_all | solution.py:155
  254.5 12.0 %all-to-all-start.1 = ((bf16[2,8,6144]{2,1,0:T(8,128)(2,1)}), bf16[2,8,6144]{2,1,0:T(8,128)(2,1)S(1)}, u32[]{:S(2)}, u32[]{:S(2)}) async-start(bf16[2,8,6144]{2,1,0:T(8,128)(2,1)} %bitcast.14), calls=%async_computation.3 | async-start | bytes 393216 | tf_op jit(solution)/shard_map/all_to_all | solution.py:154
  258.0 17.9 %copy-start.1 = (bf16[16,6144]{1,0:T(8,128)(2,1)S(1)}, bf16[16,6144]{1,0:T(8,128)(2,1)}, u32[]{:S(2)}) copy-start(bf16[16,6144]{1,0:T(8,128)(2,1)} %param.7) | copy-start | bytes 589828
  266.6 8.2 %all-to-all-start.3 = ((bf16[2,8,6144]{2,1,0:T(8,128)(2,1)}), bf16[2,8,6144]{2,1,0:T(8,128)(2,1)S(1)}, u32[]{:S(2)}, u32[]{:S(2)}) async-start(bf16[2,8,6144]{2,1,0:T(8,128)(2,1)} %bitcast.20), calls=%async_computation.7 | async-start | bytes 393216 | tf_op jit(solution)/shard_map/all_to_all | solution.py:154
Sparse Core Ops, SparseCore 0:
  37.9 44.5 reduce-scatter.4
  85.5 26.4 reduce-scatter.8
  114.1 26.5 all-gather.2
  142.7 45.3 all-gather.4
  191.1 21.9 reduce-scatter.6
  216.3 23.2 reduce-scatter.10

commit v2 on v1

--- a/solution.py
+++ b/solution.py
@@ -129,19 +129,169 @@
     )(send)
 
 
-def width_sums(term_fn, total_rows):
-    return lax.psum_scatter(
-        term_fn(jnp.int32(0), total_rows // lax.axis_size("dp") * lax.axis_size("dp")).astype(
-            jnp.bfloat16
+LAG = 2
+
+
+def chain_kernel(
+    n, x_ref, g_ref, wg_ref, wu_ref, wd_ref, act_ref, vg, vu, vd, rbuf, sbuf, acc, wsem, rs_s, rs_r, ag_s, ag_r
+):
+    d, e, t = lax.axis_index("dp"), lax.axis_index("expert"), lax.axis_index("tensor")
+    n_chunks, hc = vd.shape[0], vd.shape[1]
+    half = x_ref.shape[0] // 2
+
+    @pl.when(d > 0)
+    def _():
+        pl.semaphore_signal(
+            pltpu.get_barrier_semaphore(), inc=1, device_id=(d - 1, e, t), device_id_type=MESH
+        )
+
+    @pl.when(d < n - 1)
+    def _():
+        pl.semaphore_signal(
+            pltpu.get_barrier_semaphore(), inc=1, device_id=(d + 1, e, t), device_id_type=MESH
+        )
+
+    def loads(c):
+        cols = pl.ds(pl.multiple_of(c * hc, 128), hc)
+        return (
+            pltpu.make_async_copy(wg_ref.at[:, cols], vg.at[c], wsem.at[0, c]),
+            pltpu.make_async_copy(wu_ref.at[:, cols], vu.at[c], wsem.at[1, c]),
+            pltpu.make_async_copy(wd_ref.at[cols, :], vd.at[c], wsem.at[2, c]),
+        )
+
+    @pl.loop(0, n_chunks)
+    def _(c):
+        for copy in loads(c):
+            copy.start()
+
+    @pl.when((d > 0) & (d < n - 1))
+    def _():
+        pl.semaphore_wait(pltpu.get_barrier_semaphore(), 2)
+
+    @pl.when((d == 0) | (d == n - 1))
+    def _():
+        pl.semaphore_wait(pltpu.get_barrier_semaphore(), 1)
+
+    def chain(s):
+        return (d, d - 1, d + 1) if s == 0 else (n - 1 - d, d + 1, d - 1)
+
+    def window(s, c):
+        return act_ref.at[:, pl.ds(s * half, half), pl.ds(pl.multiple_of(c * hc, 128), hc)]
+
+    def up_copy(s, c):
+        up = chain(s)[1]
+        return remote(sbuf.at[s, c], rbuf.at[s, c], rs_s.at[s, c], rs_r.at[s, c], (up, e, t))
+
+    def down_copy(s, c):
+        down = chain(s)[2]
+        return remote(window(s, c), window(s, c), ag_s.at[s, c], ag_r.at[s, c], (down, e, t))
+
+    def spread_step(s, i):
+        p = chain(s)[0]
+        c = i - LAG * (n - 1) - LAG * p
+
+        @pl.when((p > 0) & (c >= 0) & (c < n_chunks))
+        def _():
+            down_copy(s, c).wait_recv()
+
+            @pl.when(p < n - 1)
+            def _():
+                down_copy(s, c).start()
+
+    def sum_step(s, i):
+        p = chain(s)[0]
+        c = i - LAG * (n - 1 - p)
+
+        @pl.when((c >= 0) & (c < n_chunks))
+        def _():
+            x = x_ref[pl.ds(s * half, half), :]
+            g = g_ref[pl.ds(s * half, half), :]
+            acc[0] = jnp.dot(x, vg[c], preferred_element_type=jnp.float32)
+            acc[1] = jnp.dot(x, vu[c], preferred_element_type=jnp.float32)
+            acc[2] = lax.dot_general(
+                g, vd[c], (((1,), (1,)), ((), ())), preferred_element_type=jnp.float32
+            )
+
+            @pl.when(p < n - 1)
+            def _():
+                up_copy(s, c).wait_recv()
+                acc[...] += rbuf[s, c].astype(jnp.float32)
+
+            @pl.when(p > 0)
+            def _():
+                sbuf[s, c] = acc[...].astype(jnp.bfloat16)
+                up_copy(s, c).start()
+
+            @pl.when(p == 0)
+            def _():
+                gate, upper, dhidden = acc[0], acc[1], acc[2]
+                sigma = jax.nn.sigmoid(gate)
+                active = gate * sigma
+                rows = pl.ds(s * half, half)
+                cols = pl.ds(pl.multiple_of(c * hc, 128), hc)
+                act_ref[0, rows, cols] = (active * upper).astype(jnp.bfloat16)
+                act_ref[1, rows, cols] = (
+                    dhidden * upper * sigma * (1.0 + gate * (1.0 - sigma))
+                ).astype(jnp.bfloat16)
+                act_ref[2, rows, cols] = (dhidden * active).astype(jnp.bfloat16)
+                down_copy(s, c).start()
+
+    @pl.loop(0, n_chunks + 2 * LAG * (n - 1))
+    def _(i):
+        @pl.when(i < n_chunks)
+        def _():
+            for copy in loads(i):
+                copy.wait()
+
+        for s in range(2):
+            spread_step(s, i)
+        for s in range(2):
+            sum_step(s, i)
+
+    @pl.loop(0, n_chunks)
+    def _(c):
+        for s in range(2):
+            p = chain(s)[0]
+
+            @pl.when(p > 0)
+            def _():
+                up_copy(s, c).wait_send()
+
+            @pl.when(p < n - 1)
+            def _():
+                down_copy(s, c).wait_send()
+
+
+def hidden_grads(x, g, wg, wu, wd, n_dp):
+    rows, quarter = x.shape
+    hidden = wg.shape[1]
+    hc = 128
+    nc = hidden // hc
+    vmem = pl.BlockSpec(memory_space=pltpu.VMEM)
+    anywhere = pl.BlockSpec(memory_space=pl.ANY)
+    return pl.pallas_call(
+        functools.partial(chain_kernel, n_dp),
+        out_shape=jax.ShapeDtypeStruct((3, rows, hidden), jnp.bfloat16),
+        in_specs=[vmem, vmem, anywhere, anywhere, anywhere],
+        out_specs=vmem,
+        scratch_shapes=[
+            pltpu.VMEM((nc, quarter, hc), jnp.bfloat16),
+            pltpu.VMEM((nc, quarter, hc), jnp.bfloat16),
+            pltpu.VMEM((nc, hc, quarter), jnp.bfloat16),
+            pltpu.VMEM((2, nc, 3, rows // 2, hc), jnp.bfloat16),
+            pltpu.VMEM((2, nc, 3, rows // 2, hc), jnp.bfloat16),
+            pltpu.VMEM((3, rows // 2, hc), jnp.float32),
+            pltpu.SemaphoreType.DMA((3, nc)),
+            pltpu.SemaphoreType.DMA((2, nc)),
+            pltpu.SemaphoreType.DMA((2, nc)),
+            pltpu.SemaphoreType.DMA((2, nc)),
+            pltpu.SemaphoreType.DMA((2, nc)),
+        ],
+        compiler_params=pltpu.CompilerParams(
+            collective_id=1, has_side_effects=True, vmem_limit_bytes=44 * 1024 * 1024
         ),
-        "dp",
-        scatter_dimension=0,
-        tiled=True,
-    ).astype(jnp.float32)
-
-
-def gather_rows(values):
-    return lax.all_gather(values, "dp", axis=0, tiled=True)
+        name="chain",
+    )(x, g, wg, wu, wd)
 
 
 def collect(partial_rows, n_exp, cap):
@@ -167,7 +317,6 @@
     gate_mat = w_gate[0]
     up_mat = w_up[0]
     down_mat = w_down[0]
-    hidden_width = gate_mat.shape[1]
     slots = jnp.arange(cap, dtype=jnp.int32)
     selector_list = []
     weight_list = []
@@ -195,38 +344,16 @@
     quarter = panels.shape[3]
     panel_rows = panels[:, :, :cap].reshape(-1, quarter)
     grad_panels = panels[:, :, cap:].reshape(-1, quarter)
-    total_rows = panel_rows.shape[0]
-
-    def forward_term(start, count):
-        gate_part = jnp.dot(panel_rows, gate_mat, preferred_element_type=jnp.float32)
-        up_part = jnp.dot(panel_rows, up_mat, preferred_element_type=jnp.float32)
-        return jnp.concatenate([gate_part, up_part], axis=1)
-
-    sums = width_sums(forward_term, total_rows)
-    gate = sums[:, :hidden_width]
-    upper = sums[:, hidden_width:]
-    sigma = jax.nn.sigmoid(gate)
-    active = gate * sigma
-    hidden = (active * upper).astype(jnp.bfloat16)
-    hidden_all = gather_rows(hidden)
+
+    hidden_all, dgate_all, dup_all = hidden_grads(
+        panel_rows, grad_panels, gate_mat, up_mat, down_mat, n_dp
+    )
     out_partial = jnp.dot(hidden_all, down_mat, preferred_element_type=jnp.float32)
     out_home = collect(out_partial, n_exp, cap)
     weighted = selector * weights[:, None, :]
     mixed = jnp.einsum(
         "wct,wcd->td", weighted, out_home.astype(jnp.float32), precision=lax.Precision.HIGHEST
     ).astype(jnp.bfloat16)
-    def backward_term(start, count):
-        return lax.dot_general(
-            grad_panels, down_mat, (((1,), (1,)), ((), ())), preferred_element_type=jnp.float32
-        )
-
-    dhidden = width_sums(backward_term, total_rows)
-    dgate = (dhidden * upper * sigma * (1.0 + gate * (1.0 - sigma))).astype(jnp.bfloat16)
-    dup = (dhidden * active).astype(jnp.bfloat16)
-    both_rows = jnp.concatenate([dgate, dup], axis=1)
-    both_all = gather_rows(both_rows)
-    dgate_all = both_all[:, :hidden_width]
-    dup_all = both_all[:, hidden_width:]
     grad_down = lax.dot_general(
         hidden_all, grad_panels, (((0,), (0,)), ((), ())), preferred_element_type=jnp.float32
     )

time: 283 us -> 216 us (0.76)
  waiting for transfers between devices: 166 us -> 27.4 us
  Pallas kernels: 20.2 us -> 109 us
  matrix products: 50.7 us -> 39.7 us
  other arithmetic: 8.23 us -> 2.8 us
    pallas_call x0 -> x1, Pallas kernels: none -> 88.2 us  [hidden_grads(): pl.pallas_call(functools.partial(chain_kernel, n_dp), out_shape=jax.Shape...]
    all_gather x2 -> x0, waiting for transfers between devices: 67.4 us -> none  [gather_rows(): return lax.all_gather(values, 'dp', axis=0, tiled=True)]
    reduce_scatter x2 -> x0, waiting for transfers between devices: 67.4 us -> none  [width_sums(): lax.psum_scatter(term_fn(jnp.int32(0), total_rows // lax.axis_size('dp')...]
    dot_general x3 -> x0, matrix products: 9.28 us -> none  [the longest x1 5.58 us: backward_term(): lax.dot_general(grad_panels, down_mat, (((1,), (1,)), ((), ())), preferre...]
    dot_general x1, matrix products: 5.79 us -> 2.67 us  [body(): jnp.dot(hidden_all, down_mat, preferred_element_type=jnp.float32)]
    convert_element_type x2 -> x0, other arithmetic: 3.06 us -> none  [the longest x1 1.95 us: body(): (dhidden * upper * sigma * (1.0 + gate * (1.0 - sigma))).astype(jnp.bfloa...]
    reduce_scatter x2, waiting for transfers between devices: 27.5 us -> 24.6 us  [collect(): lax.psum_scatter(partial_rows.astype(jnp.bfloat16), 'tensor', scatter_dim...]
  transfers between devices with their start and end apart: 10 -> 6, of which waited for: 7 -> 3; matrix products, arithmetic and copies ran while one was open for 19% -> 19% of each run, Pallas kernels for 0% -> 0%
where the time goes in v2:
time: 216 us
  Pallas kernels  109 us (50%)
  matrix products  39.7 us (18%)
  waiting for transfers between devices  27.4 us (13%)
  starting transfers between devices  16.8 us (8%)
  between operations  14.2 us (7%)
  local copies, waits for them, and re-layouts  5.83 us (3%)
  other arithmetic  2.8 us (1%)
    pallas_call x1, Pallas kernels, hidden_grads(): pl.pallas_call(functools.partial(chain_kernel, n_dp), out_shape=jax.Shape...  88.2 us
    reduce_scatter x2, waiting for transfers between devices, collect(): lax.psum_scatter(partial_rows.astype(jnp.bfloat16), 'tensor', scatter_dim...  24.6 us
    pallas_call x1, Pallas kernels, dispatch(): pl.pallas_call(functools.partial(dispatch_kernel, n_dp, n_exp, n_t), out_...  20.5 us
    all_to_all x2, starting transfers between devices, collect(): lax.all_to_all(local, 'dp', split_axis=1, concat_axis=2, tiled=True)  9.21 us
    dot_general x1, matrix products, body(): lax.dot_general(panel_rows, dup_all, (((0,), (0,)), ((), ())), preferred_...  7.78 us
    dot_general x1, matrix products, body(): lax.dot_general(hidden_all, grad_panels, (((0,), (0,)), ((), ())), prefer...  7.74 us
    dot_general x1, matrix products, body(): lax.dot_general(panel_rows, dgate_all, (((0,), (0,)), ((), ())), preferre...  7.74 us
    all_to_all x2, starting transfers between devices, collect(): lax.all_to_all(lax.all_to_all(local, 'dp', split_axis=1, concat_axis=2, t...  7.51 us
  transfers between devices with their start and end apart: 6, of which 3 were waited for; matrix products, arithmetic and copies ran while one was open for 19% of the time, Pallas kernels for 0%

profile of v2, /device:TPU:0, one launch (start us, length us, event | category | flops | bytes accessed | tf_op | source)
XLA Modules:
  0.0 215.5 jit_solution(10654579045680800966)
XLA Ops:
  7.2 0.0 copy-start
  7.2 0.0 reduce-scatter.3.cloned.1.call-start
  7.2 0.7 broadcast_compare_fusion.1
  7.9 0.7 multiply_reduce_fusion.1
  8.7 0.1 copy.37
  8.7 0.1 reshape.97
  8.8 0.1 reduce-window.9
  8.9 0.1 add_reduce_fusion
  9.0 0.1 sub.13
  9.1 0.1 copy.39
  9.2 0.1 copy.34
  9.2 0.1 reshape.96
  9.3 0.1 reduce-window.6
  9.4 0.1 add_reduce_fusion.1
  9.5 0.1 sub.11
  9.6 0.1 copy.36
  9.7 1.0 convert_element_type.57
  10.7 0.0 copy-done
  10.7 0.2 convolution_convert_fusion.1
  10.9 0.3 convolution_convert_fusion
  11.2 20.5 %dispatch.1 = bf16[4,8,16,1536]{3,2,1,0:T(8,128)(2,1)S(1)} custom-call(bf16[2,16,6144]{2,1,0:T(8,128)(2,1)S(1)} %pad_maximum_fusion.send_ref), custom_call_target="tpu_custom_call" | custom-call | tf_op jit(solution)/shard_map/dispatch/pallas_call | solution.py:112
  31.7 0.0 slice-start
  31.7 0.1 fusion.33
  31.8 0.0 copy-start.2
  31.8 0.0 copy-start.3
  31.9 0.0 slice-start.1
  31.9 88.2 %chain.1 = bf16[3,256,2048]{2,1,0:T(8,128)(2,1)S(1)} custom-call(bf16[256,1536]{1,0:T(8,128)(2,1)S(1)} %bitcast.66, bf16[256,1536]{1,0:T(8,128)(2,1)S(1)} %bitcast.69, bf16[1536,2048]{1,0:T(8,128)(2,1)} %bitcast.74, bf16[1536,2048]{1,0:T(8,128)(2,1)} %bitcast.75, bf16[2048,1536]{1,0:T(8,128)(2,1)} %bitcast.71), custom_call_target="tpu_custom_call" | custom-call | tf_op jit(solution)/shard_map/chain/pallas_call | solution.py:272
  120.1 0.0 copy-done.2
  120.1 0.0 copy-done.3
  120.1 0.0 slice-done
  120.1 0.0 slice-done.1
  120.1 2.7 %convolution_convert_fusion.2 = bf16[256,1536]{1,0:T(8,128)(2,1)} fusion(bf16[3,256,2048]{2,1,0:T(8,128)(2,1)S(1)} %chain.1, bf16[1,2048,1536]{2,1,0:T(8,128)(2,1)S(1)} %bitcast.73), kind=kOutput, calls=%fused_computation.11 | convolution fusion | flops 1611005952 | bytes 8126464 | tf_op jit(solution)/shard_map/dot_general | solution.py:351
  122.8 0.0 reduce-scatter.3.cloned.1.call-update
  122.8 0.0 reduce-scatter.5.cloned.1.call-start
  122.9 4.6 %fusion.6 = f32[256,1536]{1,0:T(8,128)S(1)} fusion(bf16[3,256,2048]{2,1,0:T(8,128)(2,1)S(1)} %chain.1, bf16[1,1536,2048]{2,1,0:T(8,128)(2,1)} %param.10), kind=kOutput, calls=%fused_computation.15 | convolution fusion | flops 1610612736 | bytes 8912896 | tf_op jit(solution)/shard_map/dot_general | solution.py:366
  127.5 5.7 %fusion.2 = bf16[256,1536]{1,0:T(8,128)(2,1)} fusion(f32[256,1536]{1,0:T(8,128)S(1)} %fusion.6, bf16[3,256,2048]{2,1,0:T(8,128)(2,1)S(1)} %chain.1, bf16[1,1536,2048]{2,1,0:T(8,128)(2,1)} %param.11), kind=kOutput, calls=%fused_computation.10 | convolution fusion | flops 1611399168 | bytes 9699328 | tf_op jit(solution)/shard_map/dot_general | solution.py:369
  133.2 0.0 reduce-scatter.5.cloned.1.call-update
  133.2 12.2 %reduce-scatter.3.cloned.1.call-done = bf16[64,1536]{1,0:T(8,128)(2,1)} async-done(((bf16[256,1536]{1,0:T(8,128)(2,1)}), bf16[64,1536]{1,0:T(8,128)(2,1)}) %reduce-scatter.3.cloned.1.call-update) | async-done | bytes 196624 | tf_op jit(solution)/shard_map/reduce_scatter | solution.py:300
  145.4 1.8 copy.40
  147.2 4.6 %all-to-all-start = ((bf16[2,32,1536]{2,0,1:T(2,128)(2,1)}), bf16[2,32,1536]{2,0,1:T(2,128)(2,1)S(1)}, u32[]{:S(2)}, u32[]{:S(2)}) async-start(bf16[2,32,1536]{2,0,1:T(2,128)(2,1)} %copy.40), calls=%async_computation.1 | async-start | bytes 393216 | tf_op jit(solution)/shard_map/all_to_all | solution.py:305
  151.8 7.7 %convolution_bitcast_fusion = f32[1,2048,1536]{2,1,0:T(8,128)} fusion(bf16[256,1536]{1,0:T(8,128)(2,1)} %bitcast.70, bf16[3,256,2048]{2,1,0:T(8,128)(2,1)S(1)} %chain.1), kind=kOutput, calls=%fused_computation | convolution fusion | flops 1610612736 | bytes 14417920 | tf_op jit(solution)/shard_map/dot_general | solution.py:357
  159.5 12.4 %reduce-scatter.5.cloned.1.call-done = bf16[64,1536]{1,0:T(8,128)(2,1)} async-done(((bf16[256,1536]{1,0:T(8,128)(2,1)}), bf16[64,1536]{1,0:T(8,128)(2,1)}) %reduce-scatter.5.cloned.1.call-update) | async-done | bytes 196624 | tf_op jit(solution)/shard_map/reduce_scatter | solution.py:300
  172.0 1.8 copy.42
  173.8 0.0 all-to-all-done
  173.8 4.6 %all-to-all-start.2 = ((bf16[2,32,1536]{2,0,1:T(2,128)(2,1)}), bf16[2,32,1536]{2,0,1:T(2,128)(2,1)S(1)}, u32[]{:S(2)}, u32[]{:S(2)}) async-start(bf16[2,32,1536]{2,0,1:T(2,128)(2,1)} %copy.42), calls=%async_computation.4 | async-start | bytes 393216 | tf_op jit(solution)/shard_map/all_to_all | solution.py:305
  178.4 7.7 %convolution_bitcast_fusion.2 = f32[1,1536,2048]{2,1,0:T(8,128)} fusion(bf16[256,1536]{1,0:T(8,128)(2,1)} %bitcast.67, bf16[3,256,2048]{2,1,0:T(8,128)(2,1)S(1)} %chain.1), kind=kOutput, calls=%fused_computation.2 | convolution fusion | flops 1610612736 | bytes 14417920 | tf_op jit(solution)/shard_map/dot_general | solution.py:360
  186.1 0.7 copy.41
  186.8 0.0 all-to-all-done.2
  186.8 4.1 %all-to-all-start.1 = ((bf16[2,8,6144]{2,1,0:T(8,128)(2,1)}), bf16[2,8,6144]{2,1,0:T(8,128)(2,1)}, u32[]{:S(2)}, u32[]{:S(2)}) async-start(bf16[2,8,6144]{2,1,0:T(8,128)(2,1)} %bitcast.78), calls=%async_computation.2 | async-start | bytes 393216 | tf_op jit(solution)/shard_map/all_to_all | solution.py:304
  190.9 0.0 copy-start.1
  190.9 7.8 %convolution_bitcast_fusion.1 = f32[1,1536,2048]{2,1,0:T(8,128)} fusion(bf16[256,1536]{1,0:T(8,128)(2,1)} %bitcast.68, bf16[3,256,2048]{2,1,0:T(8,128)(2,1)S(1)} %chain.1), kind=kOutput, calls=%fused_computation.1 | convolution fusion | flops 1610612736 | bytes 14417920 | tf_op jit(solution)/shard_map/dot_general | solution.py:363
  198.7 0.7 copy.43
  199.4 0.0 all-to-all-done.1
  199.4 3.4 %all-to-all-start.3 = ((bf16[2,8,6144]{2,1,0:T(8,128)(2,1)}), bf16[2,8,6144]{2,1,0:T(8,128)(2,1)S(1)}, u32[]{:S(2)}, u32[]{:S(2)}) async-start(bf16[2,8,6144]{2,1,0:T(8,128)(2,1)} %bitcast.23), calls=%async_computation.5 | async-start | bytes 393216 | tf_op jit(solution)/shard_map/all_to_all | solution.py:304
  202.8 2.0 fusion
  204.8 2.8 %all-to-all-done.3 = bf16[2,8,6144]{2,1,0:T(8,128)(2,1)S(1)} async-done(((bf16[2,8,6144]{2,1,0:T(8,128)(2,1)}), bf16[2,8,6144]{2,1,0:T(8,128)(2,1)S(1)}, u32[]{:S(2)}, u32[]{:S(2)}) %all-to-all-start.3) | async-done | bytes 196640 | tf_op jit(solution)/shard_map/all_to_all | solution.py:304
  207.6 1.0 fusion.1
  208.7 0.0 copy-done.1
  (4 shorter events, 0.0 us)
Async XLA Ops:
  7.2 3.5 %copy-start = (bf16[16,6144]{1,0:T(8,128)(2,1)S(1)}, bf16[16,6144]{1,0:T(8,128)(2,1)}, u32[]{:S(2)}) copy-start(bf16[16,6144]{1,0:T(8,128)(2,1)} %param.7) | copy-start | bytes 589828
  7.2 138.2 %reduce-scatter.3.cloned.1.call-start = ((), (), s32[]{:S(2)}) async-start(), calls=%async_computation.6 | async-start | bytes 983040 | tf_op jit(solution)/shard_map/reduce_scatter | solution.py:300
  31.7 88.4 %slice-start = ((s8[6291456]{0:T(1024)(128)(4,1)}), s8[4194304]{0:T(1024)(128)(4,1)S(1)}, s32[]{:S(2)}) async-start(s8[6291456]{0:T(1024)(128)(4,1)} %bitcast.72), calls=%async_computation.8 | async-start | bytes 8388608
  31.8 88.2 %copy-start.2 = (bf16[4,8,8,1536]{3,2,1,0:T(8,128)(2,1)}, bf16[4,8,8,1536]{3,2,1,0:T(8,128)(2,1)S(1)}, u32[]{:S(2)}) copy-start(bf16[4,8,8,1536]{3,2,1,0:T(8,128)(2,1)S(1)} %get-tuple-element.8) | copy-start | bytes 2359300
  31.8 88.2 %copy-start.3 = (bf16[4,8,8,1536]{3,2,1,0:T(8,128)(2,1)}, bf16[4,8,8,1536]{3,2,1,0:T(8,128)(2,1)S(1)}, u32[]{:S(2)}) copy-start(bf16[4,8,8,1536]{3,2,1,0:T(8,128)(2,1)S(1)} %get-tuple-element.7) | copy-start | bytes 2359300
  31.9 88.3 %slice-start.1 = ((s8[6291456]{0:T(1024)(128)(4,1)}), s8[2097152]{0:T(1024)(128)(4,1)S(1)}, s32[]{:S(2)}) async-start(s8[6291456]{0:T(1024)(128)(4,1)} %bitcast.72), calls=%async_computation.9 | async-start | bytes 4194304
  122.8 49.1 %reduce-scatter.5.cloned.1.call-start = ((), (), s32[]{:S(2)}) async-start(), calls=%async_computation.7 | async-start | bytes 983040 | tf_op jit(solution)/shard_map/reduce_scatter | solution.py:300
  147.2 26.6 %all-to-all-start = ((bf16[2,32,1536]{2,0,1:T(2,128)(2,1)}), bf16[2,32,1536]{2,0,1:T(2,128)(2,1)S(1)}, u32[]{:S(2)}, u32[]{:S(2)}) async-start(bf16[2,32,1536]{2,0,1:T(2,128)(2,1)} %copy.40), calls=%async_computation.1 | async-start | bytes 393216 | tf_op jit(solution)/shard_map/all_to_all | solution.py:305
  173.8 13.0 %all-to-all-start.2 = ((bf16[2,32,1536]{2,0,1:T(2,128)(2,1)}), bf16[2,32,1536]{2,0,1:T(2,128)(2,1)S(1)}, u32[]{:S(2)}, u32[]{:S(2)}) async-start(bf16[2,32,1536]{2,0,1:T(2,128)(2,1)} %copy.42), calls=%async_computation.4 | async-start | bytes 393216 | tf_op jit(solution)/shard_map/all_to_all | solution.py:305
  186.8 12.6 %all-to-all-start.1 = ((bf16[2,8,6144]{2,1,0:T(8,128)(2,1)}), bf16[2,8,6144]{2,1,0:T(8,128)(2,1)}, u32[]{:S(2)}, u32[]{:S(2)}) async-start(bf16[2,8,6144]{2,1,0:T(8,128)(2,1)} %bitcast.78), calls=%async_computation.2 | async-start | bytes 393216 | tf_op jit(solution)/shard_map/all_to_all | solution.py:304
  190.9 17.8 %copy-start.1 = (bf16[16,6144]{1,0:T(8,128)(2,1)S(1)}, bf16[16,6144]{1,0:T(8,128)(2,1)}, u32[]{:S(2)}) copy-start(bf16[16,6144]{1,0:T(8,128)(2,1)} %param.7) | copy-start | bytes 589828
  199.4 8.2 %all-to-all-start.3 = ((bf16[2,8,6144]{2,1,0:T(8,128)(2,1)}), bf16[2,8,6144]{2,1,0:T(8,128)(2,1)S(1)}, u32[]{:S(2)}, u32[]{:S(2)}) async-start(bf16[2,8,6144]{2,1,0:T(8,128)(2,1)} %bitcast.23), calls=%async_computation.5 | async-start | bytes 393216 | tf_op jit(solution)/shard_map/all_to_all | solution.py:304
Sparse Core Ops, SparseCore 0:
  122.9 22.3 reduce-scatter.2
  148.7 23.2 reduce-scatter.4

commit v3 on v2

--- a/solution.py
+++ b/solution.py
@@ -133,7 +133,8 @@
 
 
 def chain_kernel(
-    n, x_ref, g_ref, wg_ref, wu_ref, wd_ref, act_ref, vg, vu, vd, rbuf, sbuf, acc, wsem, rs_s, rs_r, ag_s, ag_r
+    n, x_ref, g_ref, wg_ref, wu_ref, wd_ref, act_ref, part_ref,
+    vgu, vd, part, rbuf, sbuf, out_acc, dx_acc, wsem, rs_s, rs_r, ag_s, ag_r
 ):
     d, e, t = lax.axis_index("dp"), lax.axis_index("expert"), lax.axis_index("tensor")
     n_chunks, hc = vd.shape[0], vd.shape[1]
@@ -154,8 +155,8 @@
     def loads(c):
         cols = pl.ds(pl.multiple_of(c * hc, 128), hc)
         return (
-            pltpu.make_async_copy(wg_ref.at[:, cols], vg.at[c], wsem.at[0, c]),
-            pltpu.make_async_copy(wu_ref.at[:, cols], vu.at[c], wsem.at[1, c]),
+            pltpu.make_async_copy(wg_ref.at[:, cols], vgu.at[c, :, pl.ds(0, hc)], wsem.at[0, c]),
+            pltpu.make_async_copy(wu_ref.at[:, cols], vgu.at[c, :, pl.ds(hc, hc)], wsem.at[1, c]),
             pltpu.make_async_copy(wd_ref.at[cols, :], vd.at[c], wsem.at[2, c]),
         )
 
@@ -204,30 +205,25 @@
 
         @pl.when((c >= 0) & (c < n_chunks))
         def _():
-            x = x_ref[pl.ds(s * half, half), :]
-            g = g_ref[pl.ds(s * half, half), :]
-            acc[0] = jnp.dot(x, vg[c], preferred_element_type=jnp.float32)
-            acc[1] = jnp.dot(x, vu[c], preferred_element_type=jnp.float32)
-            acc[2] = lax.dot_general(
-                g, vd[c], (((1,), (1,)), ((), ())), preferred_element_type=jnp.float32
-            )
+            rows = pl.ds(s * half, half)
 
             @pl.when(p < n - 1)
             def _():
                 up_copy(s, c).wait_recv()
-                acc[...] += rbuf[s, c].astype(jnp.float32)
+                part[c, rows, :] += rbuf[s, c].astype(jnp.float32)
 
             @pl.when(p > 0)
             def _():
-                sbuf[s, c] = acc[...].astype(jnp.bfloat16)
+                sbuf[s, c] = part[c, rows, :].astype(jnp.bfloat16)
                 up_copy(s, c).start()
 
             @pl.when(p == 0)
             def _():
-                gate, upper, dhidden = acc[0], acc[1], acc[2]
+                gate = part[c, rows, pl.ds(0, hc)]
+                upper = part[c, rows, pl.ds(hc, hc)]
+                dhidden = part[c, rows, pl.ds(2 * hc, hc)]
                 sigma = jax.nn.sigmoid(gate)
                 active = gate * sigma
-                rows = pl.ds(s * half, half)
                 cols = pl.ds(pl.multiple_of(c * hc, 128), hc)
                 act_ref[0, rows, cols] = (active * upper).astype(jnp.bfloat16)
                 act_ref[1, rows, cols] = (
@@ -236,18 +232,50 @@
                 act_ref[2, rows, cols] = (dhidden * active).astype(jnp.bfloat16)
                 down_copy(s, c).start()
 
+    def output_step(c):
+        cols = pl.ds(pl.multiple_of(c * hc, 128), hc)
+        out_acc[...] += jnp.dot(
+            act_ref[0, :, cols], vd[c], preferred_element_type=jnp.float32
+        )
+        both = jnp.concatenate([act_ref[1, :, cols], act_ref[2, :, cols]], axis=1)
+        dx_acc[...] += lax.dot_general(
+            both, vgu[c], (((1,), (1,)), ((), ())), preferred_element_type=jnp.float32
+        )
+
+    out_acc[...] = jnp.zeros_like(out_acc)
+    dx_acc[...] = jnp.zeros_like(dx_acc)
+
     @pl.loop(0, n_chunks + 2 * LAG * (n - 1))
     def _(i):
         @pl.when(i < n_chunks)
         def _():
             for copy in loads(i):
                 copy.wait()
+            part[i, :, pl.ds(0, 2 * hc)] = jnp.dot(
+                x_ref[...], vgu[i], preferred_element_type=jnp.float32
+            )
+            part[i, :, pl.ds(2 * hc, hc)] = lax.dot_general(
+                g_ref[...], vd[i], (((1,), (1,)), ((), ())), preferred_element_type=jnp.float32
+            )
 
         for s in range(2):
             spread_step(s, i)
         for s in range(2):
             sum_step(s, i)
 
+        @pl.when(i >= 2 * LAG * (n - 1))
+        def _():
+            output_step(i - 2 * LAG * (n - 1))
+
+    cap = part_ref.shape[1] // 2
+
+    @pl.loop(0, part_ref.shape[0])
+    def _(b):
+        rows = pl.ds(pl.multiple_of(b * cap, 8), cap)
+        part_ref[b] = jnp.concatenate([out_acc[rows, :], dx_acc[rows, :]], axis=0).astype(
+            jnp.bfloat16
+        )
+
     @pl.loop(0, n_chunks)
     def _(c):
         for s in range(2):
@@ -262,7 +290,7 @@
                 down_copy(s, c).wait_send()
 
 
-def hidden_grads(x, g, wg, wu, wd, n_dp):
+def hidden_grads(x, g, wg, wu, wd, n_dp, cap):
     rows, quarter = x.shape
     hidden = wg.shape[1]
     hc = 128
@@ -271,16 +299,20 @@
     anywhere = pl.BlockSpec(memory_space=pl.ANY)
     return pl.pallas_call(
         functools.partial(chain_kernel, n_dp),
-        out_shape=jax.ShapeDtypeStruct((3, rows, hidden), jnp.bfloat16),
+        out_shape=(
+            jax.ShapeDtypeStruct((3, rows, hidden), jnp.bfloat16),
+            jax.ShapeDtypeStruct((rows // cap, 2 * cap, quarter), jnp.bfloat16),
+        ),
         in_specs=[vmem, vmem, anywhere, anywhere, anywhere],
-        out_specs=vmem,
+        out_specs=(vmem, vmem),
         scratch_shapes=[
-            pltpu.VMEM((nc, quarter, hc), jnp.bfloat16),
-            pltpu.VMEM((nc, quarter, hc), jnp.bfloat16),
+            pltpu.VMEM((nc, quarter, 2 * hc), jnp.bfloat16),
             pltpu.VMEM((nc, hc, quarter), jnp.bfloat16),
-            pltpu.VMEM((2, nc, 3, rows // 2, hc), jnp.bfloat16),
-            pltpu.VMEM((2, nc, 3, rows // 2, hc), jnp.bfloat16),
-            pltpu.VMEM((3, rows // 2, hc), jnp.float32),
+            pltpu.VMEM((nc, rows, 3 * hc), jnp.float32),
+            pltpu.VMEM((2, nc, rows // 2, 3 * hc), jnp.bfloat16),
+            pltpu.VMEM((2, nc, rows // 2, 3 * hc), jnp.bfloat16),
+            pltpu.VMEM((rows, quarter), jnp.float32),
+            pltpu.VMEM((rows, quarter), jnp.float32),
             pltpu.SemaphoreType.DMA((3, nc)),
             pltpu.SemaphoreType.DMA((2, nc)),
             pltpu.SemaphoreType.DMA((2, nc)),
@@ -288,26 +320,129 @@
             pltpu.SemaphoreType.DMA((2, nc)),
         ],
         compiler_params=pltpu.CompilerParams(
-            collective_id=1, has_side_effects=True, vmem_limit_bytes=44 * 1024 * 1024
+            collective_id=1, has_side_effects=True, vmem_limit_bytes=54 * 1024 * 1024
         ),
         name="chain",
     )(x, g, wg, wu, wd)
 
 
-def collect(partial_rows, n_exp, cap):
-    n_dp = lax.axis_size("dp")
-    quarter = partial_rows.shape[1]
-    summed = lax.psum_scatter(
-        partial_rows.astype(jnp.bfloat16), "tensor", scatter_dimension=0, tiled=True
-    )
-    local = summed.reshape(n_exp, n_dp * cap, quarter)
-    return lax.all_to_all(
-        lax.all_to_all(local, "dp", split_axis=1, concat_axis=2, tiled=True),
-        "expert",
-        split_axis=0,
-        concat_axis=0,
-        tiled=True,
-    )
+def collect_kernel(
+    n_dp, n_exp, n_t, part_ref, home_ref, in_a, pair, in_b, total, a_s, a_r, b_s, b_r, c_s, c_r
+):
+    d, e, t = lax.axis_index("dp"), lax.axis_index("expert"), lax.axis_index("tensor")
+    width = part_ref.shape[3]
+    core = lax.rem(t, 2)
+    mate = t + 1 - 2 * core
+    n_hi = n_t // 2
+    offsets = [(dd, de) for dd in range(n_dp) for de in range(n_exp)]
+    offsets = offsets[1:] + offsets[:1]
+    last = len(offsets) - 1
+
+    def source(k):
+        dd, de = offsets[k]
+        return lax.rem(e + de, n_exp) * n_dp + lax.rem(d + dd, n_dp)
+
+    barrier = pltpu.get_barrier_semaphore()
+    for dd, de in offsets[:-1]:
+        pl.semaphore_signal(
+            barrier,
+            inc=1,
+            device_id=(lax.rem(d + dd, n_dp), lax.rem(e + de, n_exp), t),
+            device_id_type=MESH,
+        )
+    for peer in [lax.rem(t + 2 * j, n_t) for j in range(1, n_hi)] + [mate]:
+        pl.semaphore_signal(barrier, inc=1, device_id=(d, e, peer), device_id_type=MESH)
+    pl.semaphore_wait(barrier, last + n_hi)
+
+    order = list(range(1, n_hi)) + [0]
+    swaps = {}
+    for j in order:
+        swaps[j] = remote(
+            part_ref.at[lax.rem(mate + 2 * j, n_t)],
+            in_a.at[j],
+            a_s.at[j],
+            a_r.at[j],
+            (d, e, mate),
+        )
+        swaps[j].start()
+    sums = []
+    for j in order[:-1]:
+        swaps[j].wait_recv()
+        peer = lax.rem(t + 2 * j, n_t)
+        for k in range(last + 1):
+            where = source(k)
+            pair[j - 1, k] = (
+                part_ref[peer, where].astype(jnp.float32) + in_a[j, where].astype(jnp.float32)
+            ).astype(jnp.bfloat16)
+            copy = remote(
+                pair.at[j - 1, k],
+                in_b.at[j - 1, k],
+                b_s.at[j - 1, k],
+                b_r.at[j - 1, k],
+                (d, e, peer),
+            )
+            copy.start()
+            sums.append(copy)
+    swaps[0].wait_recv()
+    homes = []
+    for k in range(last + 1):
+        where = source(k)
+        value = part_ref[t, where].astype(jnp.float32) + in_a[0, where].astype(jnp.float32)
+        for j in order[:-1]:
+            sums[(j - 1) * (last + 1) + k].wait_recv()
+            value = value + in_b[j - 1, k].astype(jnp.float32)
+        columns = pl.ds(pl.multiple_of(d * width, 128), width)
+        if k == last:
+            home_ref[e, :, columns] = value.astype(jnp.bfloat16)
+        else:
+            total[k] = value.astype(jnp.bfloat16)
+            dd, de = offsets[k]
+            copy = remote(
+                total.at[k],
+                home_ref.at[e, :, columns],
+                c_s.at[k],
+                c_r.at[k],
+                (lax.rem(d + dd, n_dp), lax.rem(e + de, n_exp), t),
+            )
+            copy.start()
+            homes.append(copy)
+    for k in range(last):
+        dd, de = offsets[k]
+        from_dp, from_exp = lax.rem(d + n_dp - dd, n_dp), lax.rem(e + n_exp - de, n_exp)
+        columns = pl.ds(pl.multiple_of(from_dp * width, 128), width)
+        remote(
+            total.at[k], home_ref.at[from_exp, :, columns], c_s.at[k], c_r.at[k], (d, e, mate)
+        ).wait_recv()
+    for copy in list(swaps.values()) + sums + homes:
+        copy.wait_send()
+
+
+def collect(part, n_dp, n_exp, n_t):
+    rows, width = part.shape[2], part.shape[3]
+    sources, n_hi = n_dp * n_exp, n_t // 2
+    vmem = pl.BlockSpec(memory_space=pltpu.VMEM)
+    return pl.pallas_call(
+        functools.partial(collect_kernel, n_dp, n_exp, n_t),
+        out_shape=jax.ShapeDtypeStruct((n_exp, rows, n_dp * width), jnp.bfloat16),
+        in_specs=[vmem],
+        out_specs=vmem,
+        scratch_shapes=[
+            pltpu.VMEM((n_hi, sources, rows, width), jnp.bfloat16),
+            pltpu.VMEM((n_hi - 1, sources, rows, width), jnp.bfloat16),
+            pltpu.VMEM((n_hi - 1, sources, rows, width), jnp.bfloat16),
+            pltpu.VMEM((sources - 1, rows, width), jnp.bfloat16),
+            pltpu.SemaphoreType.DMA((n_hi,)),
+            pltpu.SemaphoreType.DMA((n_hi,)),
+            pltpu.SemaphoreType.DMA((n_hi - 1, sources)),
+            pltpu.SemaphoreType.DMA((n_hi - 1, sources)),
+            pltpu.SemaphoreType.DMA((sources - 1,)),
+            pltpu.SemaphoreType.DMA((sources - 1,)),
+        ],
+        compiler_params=pltpu.CompilerParams(
+            collective_id=2, has_side_effects=True, vmem_limit_bytes=32 * 1024 * 1024
+        ),
+        name="collect",
+    )(part)
 
 
 def body(tokens, expert_ids, gate_values, w_gate, w_up, w_down, grad_out):
@@ -345,11 +480,10 @@
     panel_rows = panels[:, :, :cap].reshape(-1, quarter)
     grad_panels = panels[:, :, cap:].reshape(-1, quarter)
 
-    hidden_all, dgate_all, dup_all = hidden_grads(
-        panel_rows, grad_panels, gate_mat, up_mat, down_mat, n_dp
-    )
-    out_partial = jnp.dot(hidden_all, down_mat, preferred_element_type=jnp.float32)
-    out_home = collect(out_partial, n_exp, cap)
+    acts, part = hidden_grads(panel_rows, grad_panels, gate_mat, up_mat, down_mat, n_dp, cap)
+    hidden_all, dgate_all, dup_all = acts
+    home = collect(part.reshape(panels.shape), n_dp, n_exp, n_t)
+    out_home, back_home = home[:, :cap], home[:, cap:]
     weighted = selector * weights[:, None, :]
     mixed = jnp.einsum(
         "wct,wcd->td", weighted, out_home.astype(jnp.float32), precision=lax.Precision.HIGHEST
@@ -363,13 +497,6 @@
     grad_up = lax.dot_general(
         panel_rows, dup_all, (((0,), (0,)), ((), ())), preferred_element_type=jnp.float32
     )
-    dx_partial = lax.dot_general(
-        dgate_all, gate_mat, (((1,), (1,)), ((), ())), preferred_element_type=jnp.float32
-    )
-    dx_partial = dx_partial + lax.dot_general(
-        dup_all, up_mat, (((1,), (1,)), ((), ())), preferred_element_type=jnp.float32
-    )
-    back_home = collect(dx_partial, n_exp, cap)
     grad_tokens = jnp.einsum(
         "wct,wcd->td", selector, back_home.astype(jnp.float32), precision=lax.Precision.HIGHEST
     ).astype(jnp.bfloat16)

time: 216 us -> 160 us (0.74)
  waiting for transfers between devices: 27.4 us -> 0 us
  Pallas kernels: 109 us -> 128 us
  starting transfers between devices: 16.8 us -> 0 us
  matrix products: 39.7 us -> 23.8 us
  between operations: 14.2 us -> 0.73 us
  local copies, waits for them, and re-layouts: 5.83 us -> 3.36 us
    reduce_scatter x2 -> x0, waiting for transfers between devices: 24.6 us -> none  [collect(): lax.psum_scatter(partial_rows.astype(jnp.bfloat16), 'tensor', scatter_dim...]
    pallas_call x1 -> x2, Pallas kernels: 88.2 us -> 108 us  [the longest x1 91.5 us: hidden_grads(): pl.pallas_call(functools.partial(chain_kernel, n_dp), out_shape=(jax.Shap...]
    all_to_all x4 -> x0, starting transfers between devices: 16.7 us -> none  [the longest x2 9.21 us: collect(): lax.all_to_all(local, 'dp', split_axis=1, concat_axis=2, tiled=True)]
    dot_general x3 -> x0, matrix products: 13 us -> none  [the longest x1 5.72 us: body(): lax.dot_general(dup_all, up_mat, (((1,), (1,)), ((), ())), preferred_elem...]
    reshape x3 -> x1, local copies, waits for them, and re-layouts: 3.68 us -> 0.07 us  [the longest x2 3.61 us: collect(): local = summed.reshape(n_exp, n_dp * cap, quarter)]
    all_to_all x4 -> x0, waiting for transfers between devices: 2.84 us -> none  [the longest x2 2.83 us: collect(): lax.all_to_all(lax.all_to_all(local, 'dp', split_axis=1, concat_axis=2, t...]
  transfers between devices with their start and end apart: 6 -> 0, of which waited for: 3 -> 0; matrix products, arithmetic and copies ran while one was open for 19% -> 0% of each run, Pallas kernels for 0% -> 0%
where the time goes in v3:
time: 160 us; the launch traced here: 159 us
  Pallas kernels  128 us (80%)
  matrix products  23.8 us (15%)
  local copies, waits for them, and re-layouts  3.36 us (2%)
  other arithmetic  2.8 us (2%)
    pallas_call x1, Pallas kernels, hidden_grads(): pl.pallas_call(functools.partial(chain_kernel, n_dp), out_shape=(jax.Shap...  91.5 us
    pallas_call x1, Pallas kernels, dispatch(): pl.pallas_call(functools.partial(dispatch_kernel, n_dp, n_exp, n_t), out_...  20.2 us
    pallas_call x1, Pallas kernels, collect(): pl.pallas_call(functools.partial(collect_kernel, n_dp, n_exp, n_t), out_s...  16.7 us
    dot_general x1, matrix products, body(): lax.dot_general(hidden_all, grad_panels, (((0,), (0,)), ((), ())), prefer...  7.98 us
    dot_general x1, matrix products, body(): lax.dot_general(panel_rows, dup_all, (((0,), (0,)), ((), ())), preferred_...  6.63 us
    dot_general x1, matrix products, body(): lax.dot_general(panel_rows, dgate_all, (((0,), (0,)), ((), ())), preferre...  6.63 us

profile of v3, /device:TPU:0, one launch (start us, length us, event | category | flops | bytes accessed | tf_op | source)
XLA Modules:
  0.0 159.0 jit_solution(16419986622529455372)
XLA Ops:
  0.6 0.0 copy-start
  0.6 0.8 multiply_reduce_fusion.1
  1.4 0.7 broadcast_compare_fusion.1
  2.1 0.1 copy.27
  2.2 0.1 reshape.93
  2.3 0.1 reduce-window.9
  2.3 0.1 add_reduce_fusion
  2.4 0.1 sub.13
  2.5 0.1 copy.29
  2.6 0.1 copy.24
  2.7 0.1 reshape.92
  2.8 0.1 reduce-window.6
  2.8 0.1 add_reduce_fusion.1
  2.9 0.1 sub.11
  3.0 0.1 copy.26
  3.1 0.0 copy-done
  3.1 0.2 convolution_convert_fusion.1
  3.3 1.0 convert_element_type.51
  4.3 0.3 convolution_convert_fusion
  4.6 20.2 %dispatch.1 = bf16[4,8,16,1536]{3,2,1,0:T(8,128)(2,1)S(1)} custom-call(bf16[2,16,6144]{2,1,0:T(8,128)(2,1)S(1)} %pad_maximum_fusion.send_ref), custom_call_target="tpu_custom_call" | custom-call | tf_op jit(solution)/shard_map/dispatch/pallas_call | solution.py:112
  24.8 1.3 fusion.24
  26.1 0.0 copy-start.3
  26.1 91.5 %chain.1 = (bf16[3,256,2048]{2,1,0:T(8,128)(2,1)}, bf16[32,16,1536]{2,1,0:T(8,128)(2,1)}) custom-call(bf16[256,1536]{1,0:T(8,128)(2,1)} %bitcast.44, bf16[256,1536]{1,0:T(8,128)(2,1)} %bitcast.47, bf16[1536,2048]{1,0:T(8,128)(2,1)} %bitcast.49, bf16[1536,2048]{1,0:T(8,128)(2,1)} %bitcast.50, bf16[2048,1536]{1,0:T(8,128)(2,1)} %bitcast.51), custom_call_target="tpu_custom_call" | custom-call | tf_op jit(solution)/shard_map/chain/pallas_call | solution.py:300
  117.6 0.0 copy-start.1
  117.6 1.4 copy-done.1
  119.0 16.7 %collect.1 = bf16[2,16,6144]{2,1,0:T(8,128)(2,1)S(1)} custom-call(bf16[4,8,16,1536]{3,2,1,0:T(8,128)(2,1)S(1)} %bitcast.43), custom_call_target="tpu_custom_call" | custom-call | tf_op jit(solution)/shard_map/collect/pallas_call | solution.py:424
  135.7 1.1 fusion
  136.7 1.0 fusion.1
  137.7 0.0 copy-done.3
  137.7 0.0 copy-start.2
  137.8 0.0 copy-start.4
  137.8 8.0 %convolution_bitcast_fusion = f32[1,2048,1536]{2,1,0:T(8,128)} fusion(bf16[256,1536]{1,0:T(8,128)(2,1)S(1)} %bitcast.48, bf16[3,256,2048]{2,1,0:T(8,128)(2,1)} %get-tuple-element.8), kind=kOutput, calls=%fused_computation | convolution fusion | flops 1610612736 | bytes 14417920 | tf_op jit(solution)/shard_map/dot_general | solution.py:491
  145.7 0.0 copy-done.2
  145.7 0.0 copy-done.4
  145.7 6.6 %convolution_bitcast_fusion.1 = f32[1,1536,2048]{2,1,0:T(8,128)} fusion(bf16[256,1536]{1,0:T(8,128)(2,1)S(1)} %bitcast.45, bf16[3,256,2048]{2,1,0:T(8,128)(2,1)S(1)} %copy-done.4), kind=kOutput, calls=%fused_computation.1 | convolution fusion | flops 1610612736 | bytes 14417920 | tf_op jit(solution)/shard_map/dot_general | solution.py:497
  152.4 6.6 %convolution_bitcast_fusion.2 = f32[1,1536,2048]{2,1,0:T(8,128)} fusion(bf16[256,1536]{1,0:T(8,128)(2,1)S(1)} %bitcast.46, bf16[3,256,2048]{2,1,0:T(8,128)(2,1)S(1)} %copy-done.4), kind=kOutput, calls=%fused_computation.2 | convolution fusion | flops 1610612736 | bytes 14417920 | tf_op jit(solution)/shard_map/dot_general | solution.py:494
  (3 shorter events, 0.1 us)
Async XLA Ops:
  0.6 2.5 %copy-start = (bf16[16,6144]{1,0:T(8,128)(2,1)S(1)}, bf16[16,6144]{1,0:T(8,128)(2,1)}, u32[]{:S(2)}) copy-start(bf16[16,6144]{1,0:T(8,128)(2,1)} %param.7) | copy-start | bytes 589828
  26.1 111.7 %copy-start.3 = (bf16[4,8,8,1536]{3,2,1,0:T(8,128)(2,1)S(1)}, bf16[4,8,8,1536]{3,2,1,0:T(8,128)(2,1)}, u32[]{:S(2)}) copy-start(bf16[4,8,8,1536]{3,2,1,0:T(8,128)(2,1)} %get-tuple-element.11) | copy-start | bytes 2359300
  117.6 1.4 copy-start.1
  137.7 8.0 %copy-start.2 = (bf16[4,8,8,1536]{3,2,1,0:T(8,128)(2,1)S(1)}, bf16[4,8,8,1536]{3,2,1,0:T(8,128)(2,1)}, u32[]{:S(2)}) copy-start(bf16[4,8,8,1536]{3,2,1,0:T(8,128)(2,1)} %get-tuple-element.12) | copy-start | bytes 2359300
  137.8 8.0 %copy-start.4 = (bf16[3,256,2048]{2,1,0:T(8,128)(2,1)S(1)}, bf16[3,256,2048]{2,1,0:T(8,128)(2,1)}, u32[]{:S(2)}) copy-start(bf16[3,256,2048]{2,1,0:T(8,128)(2,1)} %get-tuple-element.8) | copy-start | bytes 9437188

commit v4 on v3

--- a/solution.py
+++ b/solution.py
@@ -445,6 +445,38 @@
     )(part)
 
 
+def grads_kernel(n, left_ref, *refs):
+    for right_ref, out_ref in zip(refs[:n], refs[n:]):
+        out_ref[...] = lax.dot_general(
+            left_ref[...],
+            right_ref[...],
+            (((0,), (0,)), ((), ())),
+            preferred_element_type=jnp.float32,
+        )
+
+
+def weight_grads(left, rights):
+    depth, rows = left.shape
+    columns = rights[0].shape[1]
+    tile = 256
+    n = len(rights)
+    whole = pl.BlockSpec((depth, columns), lambda i: (0, 0))
+    return pl.pallas_call(
+        functools.partial(grads_kernel, n),
+        grid=(rows // tile,),
+        out_shape=[jax.ShapeDtypeStruct((rows, columns), jnp.float32)] * n,
+        in_specs=[pl.BlockSpec((depth, tile), lambda i: (0, i))] + [whole] * n,
+        out_specs=[pl.BlockSpec((tile, columns), lambda i: (i, 0))] * n,
+        compiler_params=pltpu.CompilerParams(vmem_limit_bytes=40 * 1024 * 1024),
+        cost_estimate=pl.CostEstimate(
+            flops=2 * n * depth * rows * columns,
+            bytes_accessed=4 * n * rows * columns,
+            transcendentals=0,
+        ),
+        name="weight_grads",
+    )(left, *rights)
+
+
 def body(tokens, expert_ids, gate_values, w_gate, w_up, w_down, grad_out):
     tok_rows = tokens.shape[0]
     cap = tok_rows // 2
@@ -488,15 +520,8 @@
     mixed = jnp.einsum(
         "wct,wcd->td", weighted, out_home.astype(jnp.float32), precision=lax.Precision.HIGHEST
     ).astype(jnp.bfloat16)
-    grad_down = lax.dot_general(
-        hidden_all, grad_panels, (((0,), (0,)), ((), ())), preferred_element_type=jnp.float32
-    )
-    grad_gate = lax.dot_general(
-        panel_rows, dgate_all, (((0,), (0,)), ((), ())), preferred_element_type=jnp.float32
-    )
-    grad_up = lax.dot_general(
-        panel_rows, dup_all, (((0,), (0,)), ((), ())), preferred_element_type=jnp.float32
-    )
+    (grad_down,) = weight_grads(hidden_all, [grad_panels])
+    grad_gate, grad_up = weight_grads(panel_rows, [dgate_all, dup_all])
     grad_tokens = jnp.einsum(
         "wct,wcd->td", selector, back_home.astype(jnp.float32), precision=lax.Precision.HIGHEST
     ).astype(jnp.bfloat16)

time: 160 us -> 156 us (0.975)
  matrix products: 23.8 us -> 2.54 us
  Pallas kernels: 128 us -> 144 us
  local copies, waits for them, and re-layouts: 3.36 us -> 5.7 us
    dot_general x3 -> x0, matrix products: 21.3 us -> none  [the longest x1 7.98 us: body(): lax.dot_general(hidden_all, grad_panels, (((0,), (0,)), ((), ())), prefer...]
    pallas_call x0 -> x2, Pallas kernels: none -> 15.6 us  [weight_grads(): pl.pallas_call(functools.partial(grads_kernel, n), grid=(rows // tile,),...]
    another operation x1 -> x2, local copies, waits for them, and re-layouts: 0.07 us -> 2.33 us  [the longest x1 2.26 us: body(): hidden_all, dgate_all, dup_all = acts]
where the time goes in v4:
time: 156 us
  Pallas kernels  144 us (92%)
  local copies, waits for them, and re-layouts  5.7 us (4%)
  other arithmetic  2.8 us (2%)
  matrix products  2.54 us (2%)
    pallas_call x1, Pallas kernels, hidden_grads(): pl.pallas_call(functools.partial(chain_kernel, n_dp), out_shape=(jax.Shap...  91.1 us
    pallas_call x1, Pallas kernels, dispatch(): pl.pallas_call(functools.partial(dispatch_kernel, n_dp, n_exp, n_t), out_...  20.5 us
    pallas_call x1, Pallas kernels, collect(): pl.pallas_call(functools.partial(collect_kernel, n_dp, n_exp, n_t), out_s...  16.7 us
    pallas_call x2, Pallas kernels, weight_grads(): pl.pallas_call(functools.partial(grads_kernel, n), grid=(rows // tile,),...  15.6 us

profile of v4, /device:TPU:0, one launch (start us, length us, event | category | flops | bytes accessed | tf_op | source)
XLA Modules:
  0.0 155.7 jit_solution(4375259245258205344)
XLA Ops:
  0.6 0.0 copy-start
  0.6 1.0 convert_element_type.51
  1.6 0.7 multiply_reduce_fusion.1
  2.4 0.7 broadcast_compare_fusion.1
  3.1 0.1 copy.27
  3.1 0.1 reshape.93
  3.2 0.1 reduce-window.9
  3.3 0.1 add_reduce_fusion
  3.4 0.1 sub.13
  3.5 0.1 copy.29
  3.6 0.1 copy.24
  3.6 0.1 reshape.92
  3.7 0.1 reduce-window.6
  3.8 0.1 add_reduce_fusion.1
  3.9 0.1 sub.11
  4.0 0.1 copy.26
  4.1 0.3 convolution_convert_fusion
  4.4 0.0 copy-done
  4.4 0.2 convolution_convert_fusion.1
  4.6 20.5 %dispatch.1 = bf16[4,8,16,1536]{3,2,1,0:T(8,128)(2,1)S(1)} custom-call(bf16[2,16,6144]{2,1,0:T(8,128)(2,1)S(1)} %pad_maximum_fusion.send_ref), custom_call_target="tpu_custom_call" | custom-call | tf_op jit(solution)/shard_map/dispatch/pallas_call | solution.py:112
  25.1 1.3 fusion.18
  26.4 91.1 %chain.1 = (bf16[3,256,2048]{2,1,0:T(8,128)(2,1)}, bf16[32,16,1536]{2,1,0:T(8,128)(2,1)}) custom-call(bf16[256,1536]{1,0:T(8,128)(2,1)} %bitcast.36, bf16[256,1536]{1,0:T(8,128)(2,1)} %bitcast.34, bf16[1536,2048]{1,0:T(8,128)(2,1)} %bitcast.40, bf16[1536,2048]{1,0:T(8,128)(2,1)} %bitcast.41, bf16[2048,1536]{1,0:T(8,128)(2,1)} %bitcast.42), custom_call_target="tpu_custom_call" | custom-call | tf_op jit(solution)/shard_map/chain/pallas_call | solution.py:300
  117.5 0.0 copy-start.3
  117.5 0.0 copy-start.4
  117.5 1.5 copy-done.4
  119.0 16.7 %collect.1 = bf16[2,16,6144]{2,1,0:T(8,128)(2,1)S(1)} custom-call(bf16[4,8,16,1536]{3,2,1,0:T(8,128)(2,1)S(1)} %bitcast.38), custom_call_target="tpu_custom_call" | custom-call | tf_op jit(solution)/shard_map/collect/pallas_call | solution.py:424
  135.7 1.0 fusion
  136.7 1.0 fusion.1
  137.8 2.3 %slice_bitcast_fusion = (bf16[256,2048]{1,0:T(8,128)(2,1)S(1)}, bf16[256,2048]{1,0:T(8,128)(2,1)S(1)}, bf16[256,2048]{1,0:T(8,128)(2,1)S(1)}) fusion(bf16[3,256,2048]{2,1,0:T(8,128)(2,1)} %get-tuple-element.10), kind=kLoop, calls=%fused_computation.6 | loop fusion | bytes 6291456 | tf_op jit(solution)/shard_map/unstack | solution.py:516
  140.1 0.0 copy-start.2
  140.1 0.0 copy-done.3
  140.1 8.9 %weight_grads.2 = (f32[1536,2048]{1,0:T(8,128)}, f32[1536,2048]{1,0:T(8,128)}) custom-call(bf16[256,1536]{1,0:T(8,128)(2,1)S(1)} %bitcast.37, bf16[256,2048]{1,0:T(8,128)(2,1)S(1)} %get-tuple-element.17.refs_0_, bf16[256,2048]{1,0:T(8,128)(2,1)S(1)} %get-tuple-element.16.refs_1_), custom_call_target="tpu_custom_call" | custom-call | flops 3221225472 | bytes 25165824 | tf_op jit(solution)/shard_map/weight_grads/pallas_call | solution.py:464
  149.0 0.0 copy-start.1
  149.0 0.0 copy-done.2
  149.0 6.7 %weight_grads.3 = f32[2048,1536]{1,0:T(8,128)} custom-call(bf16[256,2048]{1,0:T(8,128)(2,1)S(1)} %get-tuple-element.15.left_ref, bf16[256,1536]{1,0:T(8,128)(2,1)S(1)} %bitcast.35), custom_call_target="tpu_custom_call" | custom-call | flops 1610612736 | bytes 12582912 | tf_op jit(solution)/shard_map/weight_grads/pallas_call | solution.py:464
  155.7 0.0 copy-done.1
  (3 shorter events, 0.1 us)
Async XLA Ops:
  0.6 3.7 %copy-start = (bf16[16,6144]{1,0:T(8,128)(2,1)S(1)}, bf16[16,6144]{1,0:T(8,128)(2,1)}, u32[]{:S(2)}) copy-start(bf16[16,6144]{1,0:T(8,128)(2,1)} %param.7) | copy-start | bytes 589828
  117.5 22.6 %copy-start.3 = (bf16[4,8,8,1536]{3,2,1,0:T(8,128)(2,1)S(1)}, bf16[4,8,8,1536]{3,2,1,0:T(8,128)(2,1)}, u32[]{:S(2)}) copy-start(bf16[4,8,8,1536]{3,2,1,0:T(8,128)(2,1)} %get-tuple-element.19) | copy-start | bytes 2359300
  117.5 1.5 copy-start.4
  140.1 8.9 %copy-start.2 = (bf16[4,8,8,1536]{3,2,1,0:T(8,128)(2,1)S(1)}, bf16[4,8,8,1536]{3,2,1,0:T(8,128)(2,1)}, u32[]{:S(2)}) copy-start(bf16[4,8,8,1536]{3,2,1,0:T(8,128)(2,1)} %get-tuple-element.18) | copy-start | bytes 2359300
  149.0 6.7 %copy-start.1 = (bf16[16,6144]{1,0:T(8,128)(2,1)S(1)}, bf16[16,6144]{1,0:T(8,128)(2,1)}, u32[]{:S(2)}) copy-start(bf16[16,6144]{1,0:T(8,128)(2,1)} %param.7) | copy-start | bytes 589828
